TPU v7x, 128 devices: a whole 4x4x4 slice. The times are simulated.
128 devices in a mesh: fsdp: 8 (over z, x_hi), seq: 16 (over y, x_lo, core).
Axes of the slice: x: 4 (x_hi: 2, x_lo: 2; x = x_hi * 2 + x_lo), y: 4, z: 4, core: 2. Of those that a mesh axis runs over, the one named last changes fastest.
Arguments:
- tokens: bfloat16 [16384, 1024], P(('fsdp', 'seq')), may hold values from -6 to 6
- image_ids: int32 [16384], P(('fsdp', 'seq')), may hold values from 0 to 7, as said below
- valid: int32 [16384], P(('fsdp', 'seq')), may hold values from 0 to 1, as said below
- w_qkv: bfloat16 [1, 1024, 3072], P(None, 'fsdp'), may hold values from -0.1875 to 0.1875
- w_proj: bfloat16 [1, 1024, 1024], P(None, 'fsdp'), may hold values from -1.5 to 1.5
- w_fc1: bfloat16 [1, 1024, 4096], P(None, 'fsdp'), may hold values from -0.1875 to 0.1875
- w_fc2: bfloat16 [1, 4096, 1024], P(None, 'fsdp'), may hold values from -0.09375 to 0.09375
- norm_gain: bfloat16 [1, 2, 1024], P(None, None, 'fsdp'), may hold values from 0.5 to 1.5
- shifts: bfloat16 [1, 6, 1024], P(None, None, 'fsdp'), may hold values from -1.1953125 to 1.1953125
- layer_scale: bfloat16 [1, 2, 1024], P(None, None, 'fsdp'), may hold values from 0.29882812 to 1.1953125
- fc1_bias: bfloat16 [1, 4096], P(None, 'fsdp'), may hold values from -1.1953125 to 1.1953125
- grad_out: bfloat16 [16384, 1024], P(('fsdp', 'seq')), may hold values from -6 to 6
Outputs:
- result: bfloat16 [16384, 1024], P(('fsdp', 'seq'))
- grad_tokens: float32 [16384, 1024], P(('fsdp', 'seq'))
- grad_w_qkv: float32 [1, 1024, 3072], P(None, 'fsdp')
- grad_w_proj: float32 [1, 1024, 1024], P(None, 'fsdp')
- grad_w_fc1: float32 [1, 1024, 4096], P(None, 'fsdp')
- grad_w_fc2: float32 [1, 4096, 1024], P(None, 'fsdp')
- grad_norm_gain: float32 [1, 2, 1024], P(None, None, 'fsdp')
- grad_shifts: float32 [1, 6, 1024], P(None, None, 'fsdp')
- grad_layer_scale: float32 [1, 2, 1024], P(None, None, 'fsdp')
- grad_fc1_bias: float32 [1, 4096], P(None, 'fsdp')
Inputs may be any that keep to these rules, and one draw needn't show every extreme that they name: `image_ids`: each window of 2048 consecutive tokens holds 2048 // 1370 whole images of exactly 1370 tokens each, their tokens at arbitrary positions of the window; every image has its own id, and the window's padding tokens carry the id of one of its images. `valid`: each window has exactly 2048 % 1370 padding tokens, at arbitrary positions.
All inputs are finite; a program needn't handle non-finite values.
Results may differ from a plain program's by a relative error of at most 0.022.
Values may be sent and summed in bfloat16 or wider, within the bound.
A program may use at most 128 MiB of HBM per device.

v0:
```python
import jax
import jax.numpy as jnp
from jax import lax
from jax.sharding import PartitionSpec as P

HEAD_DIM = 64


NORM_EPS = 1e-06
NEG_FILL = -1e30


def layer_norm(values, gain, shift):
    mean_val = jnp.mean(values, axis=-1, keepdims=True)
    centered = values - mean_val
    variance = jnp.mean(centered * centered, axis=-1, keepdims=True)
    return centered * lax.rsqrt(variance + NORM_EPS) * gain + shift


def gelu_exact(pre_act):
    return 0.5 * pre_act * (1.0 + lax.erf(pre_act * 0.7071067811865476))


def contract_rows(left, right):
    return lax.dot_general(
        left, right, (((0,), (0,)), ((), ())), preferred_element_type=jnp.float32
    )


def contract_cols(left, right):
    return lax.dot_general(
        left, right, (((1,), (1,)), ((), ())), preferred_element_type=jnp.float32
    )


def block_size(rows):
    block_rows = rows
    while block_rows % 2 == 0 and block_rows // 2 >= 512:
        block_rows = block_rows // 2
    return block_rows


def fetch_layer(pieces):
    return (
        lax.all_gather(pieces[0], "fsdp", axis=0, tiled=True),
        lax.all_gather(pieces[1], "fsdp", axis=0, tiled=True),
        lax.all_gather(pieces[2], "fsdp", axis=0, tiled=True),
        lax.all_gather(pieces[3], "fsdp", axis=0, tiled=True),
        lax.all_gather(pieces[4], "fsdp", axis=1, tiled=True),
        lax.all_gather(pieces[5], "fsdp", axis=1, tiled=True),
        lax.all_gather(pieces[6], "fsdp", axis=1, tiled=True),
        lax.all_gather(pieces[7], "fsdp", axis=0, tiled=True),
    )


def refetch_layer(pieces):
    return (
        lax.all_gather(pieces[0], "fsdp", axis=0, tiled=True),
        lax.all_gather(pieces[1], "fsdp", axis=0, tiled=True),
        lax.all_gather(pieces[2], "fsdp", axis=0, tiled=True),
        lax.all_gather(pieces[3], "fsdp", axis=0, tiled=True),
        lax.all_gather(pieces[4], "fsdp", axis=1, tiled=True),
        lax.all_gather(pieces[5], "fsdp", axis=1, tiled=True),
        lax.all_gather(pieces[6], "fsdp", axis=1, tiled=True),
        lax.all_gather(pieces[7], "fsdp", axis=0, tiled=True),
    )


def reduce_terms(terms):
    shares = (
        lax.psum_scatter(
            terms[0].astype(jnp.bfloat16), "fsdp", scatter_dimension=0, tiled=True
        ).astype(jnp.float32),
        lax.psum_scatter(
            terms[1].astype(jnp.bfloat16), "fsdp", scatter_dimension=0, tiled=True
        ).astype(jnp.float32),
        lax.psum_scatter(
            terms[2].astype(jnp.bfloat16), "fsdp", scatter_dimension=0, tiled=True
        ).astype(jnp.float32),
    )
    return (
        lax.psum(shares[0].astype(jnp.bfloat16), "seq").astype(jnp.float32),
        lax.psum(shares[1].astype(jnp.bfloat16), "seq").astype(jnp.float32),
        lax.psum(shares[2].astype(jnp.bfloat16), "seq").astype(jnp.float32),
    )


def block_scores(query_blk, key_h, ids_blk, ids_all, valid_all, scale):
    raw = jnp.einsum("qhd,khd->hqk", query_blk, key_h, preferred_element_type=jnp.float32) * scale
    allowed = (ids_blk[:, None] == ids_all[None, :]) & (valid_all[None, :] == 1)
    return jnp.where(allowed[None], raw, NEG_FILL)


def attend(queries, key_rows, value_rows, ids_all, valid_all):
    rows = queries.shape[0]
    heads = queries.shape[1] // HEAD_DIM
    query_h = queries.reshape(rows, heads, HEAD_DIM)
    key_h = key_rows.reshape(rows, heads, HEAD_DIM)
    value_h = value_rows.reshape(rows, heads, HEAD_DIM)
    block_rows = block_size(rows)
    block_count = rows // block_rows
    scale = HEAD_DIM ** (-0.5)

    def one_block(block_idx):
        row_start = block_idx * block_rows
        query_blk = lax.dynamic_slice_in_dim(query_h, row_start, block_rows, 0)
        ids_blk = lax.dynamic_slice_in_dim(ids_all, row_start, block_rows, 0)
        scores = block_scores(query_blk, key_h, ids_blk, ids_all, valid_all, scale)
        row_max = jnp.max(scores, axis=-1, keepdims=True)
        exp_terms = jnp.exp(scores - row_max)
        row_total = jnp.sum(exp_terms, axis=-1, keepdims=True)
        probs_bf = (exp_terms / row_total).astype(jnp.bfloat16)
        mixed = jnp.einsum("hqk,khd->qhd", probs_bf, value_h, preferred_element_type=jnp.float32)
        return (
            mixed.astype(jnp.bfloat16).reshape(block_rows, heads * HEAD_DIM),
            (row_max + jnp.log(row_total))[:, :, 0],
        )

    blocks_out, log_sums = lax.map(one_block, jnp.arange(block_count))
    return (blocks_out.reshape(rows, heads * HEAD_DIM), log_sums)


def attend_back(queries, key_rows, value_rows, log_sums, grad_heads, ids_all, valid_all):
    rows = queries.shape[0]
    heads = queries.shape[1] // HEAD_DIM
    query_h = queries.reshape(rows, heads, HEAD_DIM)
    key_h = key_rows.reshape(rows, heads, HEAD_DIM)
    value_h = value_rows.reshape(rows, heads, HEAD_DIM)
    grad_h = grad_heads.reshape(rows, heads, HEAD_DIM)
    block_rows = block_size(rows)
    block_count = rows // block_rows
    scale = HEAD_DIM ** (-0.5)

    def one_block(carry, block_idx):
        key_acc, value_acc = carry
        row_start = block_idx * block_rows
        query_blk = lax.dynamic_slice_in_dim(query_h, row_start, block_rows, 0)
        ids_blk = lax.dynamic_slice_in_dim(ids_all, row_start, block_rows, 0)
        grad_blk = lax.dynamic_slice_in_dim(grad_h, row_start, block_rows, 0)
        lse_blk = log_sums[block_idx]
        scores = block_scores(query_blk, key_h, ids_blk, ids_all, valid_all, scale)
        probs = jnp.exp(scores - lse_blk[:, :, None])
        probs_bf = probs.astype(jnp.bfloat16)
        value_acc = value_acc + jnp.einsum(
            "hqk,qhd->khd", probs_bf, grad_blk, preferred_element_type=jnp.float32
        )
        grad_probs = jnp.einsum(
            "qhd,khd->hqk", grad_blk, value_h, preferred_element_type=jnp.float32
        )
        inner_sum = jnp.sum(probs * grad_probs, axis=-1, keepdims=True)
        grad_scores = (scale * probs * (grad_probs - inner_sum)).astype(jnp.bfloat16)
        grad_query = jnp.einsum(
            "hqk,khd->qhd", grad_scores, key_h, preferred_element_type=jnp.float32
        )
        key_acc = key_acc + jnp.einsum(
            "hqk,qhd->khd", grad_scores, query_blk, preferred_element_type=jnp.float32
        )
        return (
            (key_acc, value_acc),
            grad_query.astype(jnp.bfloat16).reshape(block_rows, heads * HEAD_DIM),
        )

    zero_acc = jnp.zeros((rows, heads, HEAD_DIM), jnp.float32)
    (key_acc, value_acc), grad_blocks = lax.scan(
        one_block, (zero_acc, zero_acc), jnp.arange(block_count)
    )
    grad_queries = grad_blocks.reshape(rows, heads * HEAD_DIM)
    grad_keys = key_acc.astype(jnp.bfloat16).reshape(rows, heads * HEAD_DIM)
    grad_values = value_acc.astype(jnp.bfloat16).reshape(rows, heads * HEAD_DIM)
    return (grad_queries, grad_keys, grad_values)


def forward_layer(residual, gathered, ids_all, valid_all):
    wqkv, wproj, wfc1, wfc2, gains, shift_rows, scales, bias_one = gathered
    gains = gains.astype(jnp.float32)
    shift_rows = shift_rows.astype(jnp.float32)
    scales = scales.astype(jnp.float32)
    width = residual.shape[1]
    normed_in = layer_norm(residual, gains[0], shift_rows[0]).astype(jnp.bfloat16)
    qkv_rows = jnp.dot(normed_in, wqkv, preferred_element_type=jnp.float32)
    queries = (qkv_rows[:, :width] + shift_rows[2]).astype(jnp.bfloat16)
    key_rows = qkv_rows[:, width : 2 * width].astype(jnp.bfloat16)
    value_rows = (qkv_rows[:, 2 * width :] + shift_rows[3]).astype(jnp.bfloat16)
    query_h, key_h, value_h = (
        lax.all_to_all(queries, "seq", split_axis=1, concat_axis=0, tiled=True),
        lax.all_to_all(key_rows, "seq", split_axis=1, concat_axis=0, tiled=True),
        lax.all_to_all(value_rows, "seq", split_axis=1, concat_axis=0, tiled=True),
    )
    attn_heads, log_sums = attend(query_h, key_h, value_h, ids_all, valid_all)
    attn_tok = lax.all_to_all(attn_heads, "seq", split_axis=0, concat_axis=1, tiled=True)
    attn_branch = jnp.dot(attn_tok, wproj, preferred_element_type=jnp.float32) + shift_rows[4]
    middle = residual + scales[0] * attn_branch
    normed_mid = layer_norm(middle, gains[1], shift_rows[1]).astype(jnp.bfloat16)
    pre_act = jnp.dot(normed_mid, wfc1, preferred_element_type=jnp.float32) + bias_one.astype(
        jnp.float32
    )
    act_bf = gelu_exact(pre_act).astype(jnp.bfloat16)
    mlp_out = jnp.dot(act_bf, wfc2, preferred_element_type=jnp.float32) + shift_rows[5]
    next_res = middle + scales[1] * mlp_out
    saved = (
        residual,
        normed_in,
        query_h,
        key_h,
        value_h,
        log_sums,
        attn_tok,
        attn_branch,
        middle,
        normed_mid,
        pre_act,
        act_bf,
        mlp_out,
    )
    return (next_res, saved)


def backward_layer(grad_res, gathered, saved, ids_all, valid_all):
    wqkv, wproj, wfc1, wfc2, gains, shift_rows, scales, bias_one = gathered
    gains = gains.astype(jnp.float32)
    shift_rows = shift_rows.astype(jnp.float32)
    scales = scales.astype(jnp.float32)
    (
        residual,
        normed_in,
        query_h,
        key_h,
        value_h,
        log_sums,
        attn_tok,
        attn_branch,
        middle,
        normed_mid,
        pre_act,
        act_bf,
        mlp_out,
    ) = saved
    grad_scale_mlp = jnp.sum(grad_res * mlp_out, axis=0)
    grad_mlp = (scales[1] * grad_res).astype(jnp.bfloat16)
    grad_fc2 = contract_rows(act_bf, grad_mlp)
    grad_bias_out = jnp.sum(grad_mlp.astype(jnp.float32), axis=0)
    grad_act = contract_cols(grad_mlp, wfc2)
    gelu_pull = jax.vjp(gelu_exact, pre_act)[1]
    grad_pre = gelu_pull(grad_act)[0].astype(jnp.bfloat16)
    grad_fc1 = contract_rows(normed_mid, grad_pre)
    grad_bias_one = jnp.sum(grad_pre.astype(jnp.float32), axis=0)
    grad_normed_mid = contract_cols(grad_pre, wfc1)
    mlp_shares = reduce_terms((grad_fc1, grad_fc2, grad_bias_one))
    mid_pull = jax.vjp(layer_norm, middle, gains[1], shift_rows[1])[1]
    grad_mid_ln, grad_gain_mid, grad_shift_mid = mid_pull(grad_normed_mid)
    grad_middle = grad_res + grad_mid_ln
    grad_scale_attn = jnp.sum(grad_middle * attn_branch, axis=0)
    grad_attn = (scales[0] * grad_middle).astype(jnp.bfloat16)
    grad_proj = contract_rows(attn_tok, grad_attn)
    grad_bias_proj = jnp.sum(grad_attn.astype(jnp.float32), axis=0)
    grad_attn_tok = contract_cols(grad_attn, wproj).astype(jnp.bfloat16)
    grad_heads = lax.all_to_all(grad_attn_tok, "seq", split_axis=1, concat_axis=0, tiled=True)
    grad_query_h, grad_key_h, grad_value_h = attend_back(
        query_h, key_h, value_h, log_sums, grad_heads, ids_all, valid_all
    )
    grad_query, grad_key, grad_value = (
        lax.all_to_all(grad_query_h, "seq", split_axis=0, concat_axis=1, tiled=True),
        lax.all_to_all(grad_key_h, "seq", split_axis=0, concat_axis=1, tiled=True),
        lax.all_to_all(grad_value_h, "seq", split_axis=0, concat_axis=1, tiled=True),
    )
    grad_qkv_rows = jnp.concatenate([grad_query, grad_key, grad_value], axis=1)
    grad_qkv = contract_rows(normed_in, grad_qkv_rows)
    grad_bias_q = jnp.sum(grad_query.astype(jnp.float32), axis=0)
    grad_bias_v = jnp.sum(grad_value.astype(jnp.float32), axis=0)
    grad_normed_in = contract_cols(grad_qkv_rows, wqkv)
    in_pull = jax.vjp(layer_norm, residual, gains[0], shift_rows[0])[1]
    grad_in_ln, grad_gain_in, grad_shift_in = in_pull(grad_normed_in)
    grad_input = grad_middle + grad_in_ln
    vector_grads = jnp.stack(
        [
            grad_gain_in,
            grad_gain_mid,
            grad_shift_in,
            grad_shift_mid,
            grad_bias_q,
            grad_bias_v,
            grad_bias_proj,
            grad_bias_out,
            grad_scale_attn,
            grad_scale_mlp,
        ],
        axis=1,
    )
    attn_shares = reduce_terms((grad_qkv, grad_proj, vector_grads))
    vector_shares = attn_shares[2].T
    layer_grads = (
        attn_shares[0],
        attn_shares[1],
        mlp_shares[0],
        mlp_shares[1],
        vector_shares[0:2],
        vector_shares[2:8],
        vector_shares[8:10],
        mlp_shares[2],
    )
    return (grad_input, layer_grads)


def body(
    tokens,
    image_ids,
    valid,
    w_qkv,
    w_proj,
    w_fc1,
    w_fc2,
    norm_gain,
    shifts,
    layer_scale,
    fc1_bias,
    grad_out,
):
    ids_all, valid_all = (
        lax.all_gather(image_ids, "seq", axis=0, tiled=True),
        lax.all_gather(valid, "seq", axis=0, tiled=True),
    )
    depth = w_qkv.shape[0]
    residual = tokens.astype(jnp.float32)
    layer_idx = 0
    pieces = (
        w_qkv[layer_idx],
        w_proj[layer_idx],
        w_fc1[layer_idx],
        w_fc2[layer_idx],
        norm_gain[layer_idx],
        shifts[layer_idx],
        layer_scale[layer_idx],
        fc1_bias[layer_idx],
    )
    gathered = fetch_layer(pieces)
    residual, saved = forward_layer(residual, gathered, ids_all, valid_all)
    kept_layers = [(pieces, gathered, saved)]
    final_out = residual.astype(jnp.bfloat16)
    grad_res = grad_out.astype(jnp.float32)
    all_grads = [None] * depth
    for layer_idx in reversed(range(depth)):
        pieces, gathered, saved = kept_layers[layer_idx]
        gathered = refetch_layer(pieces)
        grad_res, layer_grads = backward_layer(grad_res, gathered, saved, ids_all, valid_all)
        all_grads[layer_idx] = layer_grads
    stacked = [jnp.stack([all_grads[0][member]], axis=0) for member in range(8)]
    return (
        final_out,
        grad_res,
        stacked[0],
        stacked[1],
        stacked[2],
        stacked[3],
        stacked[4],
        stacked[5],
        stacked[6],
        stacked[7],
    )


def solution(mesh):
    in_specs = (
        P(("fsdp", "seq"), None),
        P(("fsdp", "seq")),
        P(("fsdp", "seq")),
        P(None, "fsdp", None),
        P(None, "fsdp", None),
        P(None, "fsdp", None),
        P(None, "fsdp", None),
        P(None, None, "fsdp"),
        P(None, None, "fsdp"),
        P(None, None, "fsdp"),
        P(None, "fsdp"),
        P(("fsdp", "seq"), None),
    )
    out_specs = (
        P(("fsdp", "seq"), None),
        P(("fsdp", "seq"), None),
        P(None, "fsdp", None),
        P(None, "fsdp", None),
        P(None, "fsdp", None),
        P(None, "fsdp", None),
        P(None, None, "fsdp"),
        P(None, None, "fsdp"),
        P(None, None, "fsdp"),
        P(None, "fsdp"),
    )
    return jax.shard_map(body, mesh=mesh, in_specs=in_specs, out_specs=out_specs, check_vma=False)
```

profile of v0, /device:TPU:1, one launch (start us, length us, event | category | flops | bytes accessed | tf_op | source)
XLA Modules:
  0.0 1066.1 jit_solution(10904996668370200404)
XLA Ops:
  10.0 21.6 %all-gather.1 = bf16[1,2,1024]{2,1,0:T(2,128)(2,1)S(1)} all-gather(bf16[1,2,128]{2,1,0:T(2,128)(2,1)S(1)} %copy-done.37), channel_id=3, replica_groups=mesh['fsdp'=8,'seq'=16] {'fsdp'}, dimensions={2}, use_global_device_ids=true | all-gather | bytes 4608 | tf_op jit(solution)/shard_map/all_gather | solution.py:49
  31.6 25.5 %all-gather.2 = bf16[1,6,1024]{2,1,0:T(8,128)(2,1)S(1)} all-gather(bf16[1,6,128]{2,1,0:T(8,128)(2,1)S(1)} %copy-done.35), channel_id=4, replica_groups=mesh['fsdp'=8,'seq'=16] {'fsdp'}, dimensions={2}, use_global_device_ids=true | all-gather | bytes 13824 | tf_op jit(solution)/shard_map/all_gather | solution.py:50
  57.5 45.1 %all-gather.15.cloned.1.call-done = bf16[1,1024,3072]{2,1,0:T(8,128)(2,1)} async-done(((bf16[1,128,3072]{2,1,0:T(8,128)(2,1)}), bf16[1,1024,3072]{2,1,0:T(8,128)(2,1)}) %all-gather.15.cloned.1.call-update) | async-done | bytes 6291472 | tf_op jit(solution)/shard_map/all_gather | solution.py:45
  102.6 3.9 fusion.41
  107.5 5.2 all-to-all-start
  113.5 8.5 all-to-all-done
  122.0 5.0 all-to-all-start.2
  127.8 6.3 all-to-all-done.2
  134.2 4.3 all-to-all-start.1
  138.5 21.3 %all-gather.8 = s32[16,1,128]{2,1,0:T(1,128)S(1)} all-gather(s32[1,1,128]{2,1,0:T(1,128)S(1)} %bitcast.280), channel_id=1, replica_groups=mesh['fsdp'=8,'seq'=16] {'seq'}, dimensions={0}, use_global_device_ids=true | all-gather | bytes 8704 | tf_op jit(solution)/shard_map/all_gather | solution.py:319
  159.8 17.3 %all-gather.9 = s32[16,1,128]{2,1,0:T(1,128)S(1)} all-gather(s32[1,1,128]{2,1,0:T(1,128)S(1)} %bitcast.281), channel_id=1, replica_groups=mesh['fsdp'=8,'seq'=16] {'seq'}, dimensions={0}, use_global_device_ids=true | all-gather | bytes 8704 | tf_op jit(solution)/shard_map/all_gather | solution.py:320
  178.0 17.6 %while.27 = (s32[]{:T(128)}, bf16[4,512,64]{1,2,0:T(8,128)(2,1)S(1)}, f32[4,1,512]{2,1,0:T(1,128)S(1)}, s32[4]{0:T(128)S(1)}, s32[2048]{0:T(1024)S(1)}, /*index=...) while((s32[]{:T(128)}, ...), condition=%wide.region_5.6_spmd, body=%wide.region_2.5_spmd.sunk | while | flops 278955520 | bytes 13285575 | solution.py:119
  196.8 3.5 all-to-all-start.3
  200.4 26.3 %all-gather.6 = bf16[1,4096]{1,0:T(2,128)(2,1)S(1)} all-gather(bf16[1,512]{1,0:T(2,128)(2,1)S(1)} %copy-done.36), channel_id=8, replica_groups=mesh['fsdp'=8,'seq'=16] {'fsdp'}, dimensions={1}, use_global_device_ids=true | all-gather | bytes 9216 | tf_op jit(solution)/shard_map/all_gather | solution.py:52
  226.7 15.8 %all-gather = bf16[1,2,1024]{2,1,0:T(2,128)(2,1)S(1)} all-gather(bf16[1,2,128]{2,1,0:T(2,128)(2,1)S(1)} %copy-done.40), channel_id=2, replica_groups=mesh['fsdp'=8,'seq'=16] {'fsdp'}, dimensions={2}, use_global_device_ids=true | all-gather | bytes 4608 | tf_op jit(solution)/shard_map/all_gather | solution.py:51
  242.6 3.0 fusion.89
  245.8 22.0 %all-gather.19.cloned.1.call-done = bf16[1,1024,4096]{2,1,0:T(8,128)(2,1)} async-done(((bf16[1,128,4096]{2,1,0:T(8,128)(2,1)}), bf16[1,1024,4096]{2,1,0:T(8,128)(2,1)}) %all-gather.19.cloned.1.call-update) | async-done | bytes 8388624 | tf_op jit(solution)/shard_map/all_gather | solution.py:47
  267.8 4.7 fusion.43
  272.6 102.5 %all-gather.21.cloned.1.call-done = bf16[1,4096,1024]{2,1,0:T(8,128)(2,1)} async-done(((bf16[1,512,1024]{2,1,0:T(8,128)(2,1)}), bf16[1,4096,1024]{2,1,0:T(8,128)(2,1)}) %all-gather.21.cloned.1.call-update) | async-done | bytes 8388624 | tf_op jit(solution)/shard_map/all_gather | solution.py:48
  375.1 7.1 fusion.94
  382.3 3.0 multiply_reduce_fusion.2
  390.6 5.4 all-to-all-start.4
  396.3 3.0 convolution_convert_fusion.4
  399.3 3.8 all-to-all-done.4
  404.2 76.5 %while.28 = (s32[]{:T(128)}, f32[2048,1,64]{0,2,1:T(8,128)}, f32[2048,1,64]{0,2,1:T(8,128)S(1)}, bf16[4,512,64]{1,2,0:T(8,128)(2,1)}, s32[4]{0:T(128)S(1)}, /*in...) while((s32[]{:T(128)}, f32[2048,1,64]{0,2,1:T(8,128)}, ...), condition=%wide.region_12.13_spmd.clone, body=%wide.region_10.12_spmd.clone.sunk | while | flops 684230144 | bytes 89232376 | solution.py:164
  405.5 2.7 fusion.131
  410.2 4.2 multiply_reduce_fusion.6
  429.1 4.3 multiply_reduce_fusion.6
  448.4 4.2 multiply_reduce_fusion.6
  467.5 4.2 multiply_reduce_fusion.6
  482.7 4.3 all-to-all-start.6
  487.8 6.4 all-to-all-done.6
  494.2 4.3 all-to-all-start.7
  499.0 6.8 all-to-all-done.7
  505.8 10.6 all_to_all.140
  516.4 4.7 convolution_convert_fusion.3
  522.3 5.8 convolution_convert_fusion.2
  529.7 4.6 convolution_convert_fusion.1
  534.5 5.4 fusion.86
  540.4 6.2 fusion.73
  549.2 67.0 %reduce-scatter.8.cloned.1.call-done = bf16[128,3072]{1,0:T(8,128)(2,1)} async-done(((bf16[1024,3072]{1,0:T(8,128)(2,1)}), bf16[128,3072]{1,0:T(8,128)(2,1)}) %reduce-scatter.8.cloned.1.call-update) | async-done | bytes 786448 | tf_op jit(solution)/shard_map/reduce_scatter | solution.py:71
  616.2 116.8 %reduce-scatter.12.cloned.1.call-done = bf16[128,4096]{1,0:T(8,128)(2,1)} async-done(((bf16[1024,4096]{1,0:T(8,128)(2,1)}), bf16[128,4096]{1,0:T(8,128)(2,1)}) %reduce-scatter.12.cloned.1.call-update) | async-done | bytes 1048592 | tf_op jit(solution)/shard_map/reduce_scatter | solution.py:71
  733.0 116.6 %reduce-scatter.14.cloned.1.call-done = bf16[512,1024]{1,0:T(8,128)(2,1)} async-done(((bf16[4096,1024]{1,0:T(8,128)(2,1)}), bf16[512,1024]{1,0:T(8,128)(2,1)}) %reduce-scatter.14.cloned.1.call-update) | async-done | bytes 1048592 | tf_op jit(solution)/shard_map/reduce_scatter | solution.py:74
  850.8 16.4 %all-reduce = bf16[4096]{0:T(1024)(128)(2,1)S(1)} all-reduce(bf16[4096]{0:T(1024)(128)(2,1)S(1)} %get-tuple-element.273), channel_id=15, replica_groups=mesh['fsdp'=8,'seq'=16] {'fsdp'}, use_global_device_ids=true, to_apply=%region_36.37.clone | all-reduce | flops 4096 | bytes 16384
  867.3 52.7 %reduce-scatter.16.cloned.1.call-done = bf16[128,10]{1,0:T(8,128)(2,1)} async-done(((bf16[1024,10]{1,0:T(8,128)(2,1)}), bf16[128,10]{1,0:T(8,128)(2,1)}) %reduce-scatter.16.cloned.1.call-update) | async-done | bytes 2576
  920.9 29.6 %all-reduce.1 = (bf16[10,128]{1,0:T(8,128)(2,1)S(1)}, bf16[1,512]{1,0:T(2,128)(2,1)S(1)}) all-reduce(bf16[10,128]{1,0:T(8,128)(2,1)S(1)} %bitcast.278, bf16[1,512]{1,0:T(2,128)(2,1)S(1)} %stack.105), channel_id=1, replica_groups=mesh['fsdp'=8,'seq'=16] {'seq'}, use_global_device_ids=true, to_apply=%region_34.35 | all-reduce | flops 1792 | bytes 7168 | tf_op jit(solution)/shard_map/psum | solution.py:84
  952.3 100.5 %all-reduce.5.cloned.1.call-done = (bf16[1,128,3072]{2,1,0:T(8,128)(2,1)}, bf16[1,128,1024]{2,1,0:T(8,128)(2,1)}, bf16[1,128,4096]{2,1,0:T(8,128)(2,1)}, bf16[1,512,1024]{2,1,0:T(8,128)(2,1)}) async-done(((bf16[1,128,3072]{2,1,0:T(8,128)(2,1)}, bf16[1,128,1024]{2,1,0:T(8,128)(2,1)}, bf16[1,128,4096]{2,1,0:T(8,128)(2,1)}, bf16[1,512,1024]{2,1,0:T(8,128)(2,1)}), (bf16[1,128,3072]{2,1,0:T(8,128)(2,1)}, ...) | async-done | bytes 3145744 | tf_op jit(solution)/shard_map/psum | solution.py:82
  1052.7 2.8 stack.88
  (294 shorter events, 91.7 us)
Async XLA Ops:
  7.2 24.4 %copy-start.35 = (bf16[1,6,128]{2,1,0:T(8,128)(2,1)S(1)}, bf16[1,6,128]{2,1,0:T(8,128)(2,1)}, u32[]{:S(2)}) copy-start(bf16[1,6,128]{2,1,0:T(8,128)(2,1)} %param.24) | copy-start | bytes 4612
  7.2 49.9 %copy-start.6 = (bf16[128,1024]{1,0:T(8,128)(2,1)S(1)}, bf16[128,1024]{1,0:T(8,128)(2,1)}, u32[]{:S(2)}) copy-start(bf16[128,1024]{1,0:T(8,128)(2,1)} %param.16) | copy-start | bytes 786436
  7.2 95.4 %all-gather.15.cloned.1.call-start = ((), (), s32[]{:S(2)}) async-start(), calls=%async_computation.17 | async-start | bytes 7077888 | tf_op jit(solution)/shard_map/all_gather | solution.py:45
  7.9 234.6 %all-gather.17.cloned.1.call-start = ((), (), s32[]{:S(2)}) async-start(), calls=%async_computation.18 | async-start | bytes 2359296 | tf_op jit(solution)/shard_map/all_gather | solution.py:46
  8.7 259.2 %all-gather.19.cloned.1.call-start = ((), (), s32[]{:S(2)}) async-start(), calls=%async_computation.19 | async-start | bytes 9437184 | tf_op jit(solution)/shard_map/all_gather | solution.py:47
  9.4 365.7 %all-gather.21.cloned.1.call-start = ((), (), s32[]{:S(2)}) async-start(), calls=%async_computation.20 | async-start | bytes 9437184 | tf_op jit(solution)/shard_map/all_gather | solution.py:48
  106.6 31.9 %copy-start.38 = (s32[128]{0:T(128)S(1)}, s32[128]{0:T(128)}, u32[]{:S(2)}) copy-start(s32[128]{0:T(128)} %param.17) | copy-start | bytes 1540
  106.6 53.1 %copy-start.39 = (s32[128]{0:T(128)S(1)}, s32[128]{0:T(128)}, u32[]{:S(2)}) copy-start(s32[128]{0:T(128)} %param.18) | copy-start | bytes 1540
  107.5 14.5 %all-to-all-start = ((bf16[128,16,64]{0,2,1:T(8,128)(2,1)}), bf16[128,16,64]{0,2,1:T(8,128)(2,1)S(1)}, u32[]{:S(2)}, u32[]{:S(2)}) async-start(bf16[128,16,64]{0,2,1:T(8,128)(2,1)} %bitcast.18), calls=%async_computation | async-start | bytes 524288 | tf_op jit(solution)/shard_map/all_to_all | solution.py:185
  122.0 12.2 %all-to-all-start.2 = ((bf16[128,16,64]{0,2,1:T(8,128)(2,1)}), bf16[128,16,64]{0,2,1:T(8,128)(2,1)S(1)}, u32[]{:S(2)}, u32[]{:S(2)}) async-start(bf16[128,16,64]{0,2,1:T(8,128)(2,1)} %bitcast.23), calls=%async_computation.2 | async-start | bytes 524288 | tf_op jit(solution)/shard_map/all_to_all | solution.py:187
  134.2 43.5 %all-to-all-start.1 = ((bf16[128,16,64]{0,2,1:T(8,128)(2,1)}), bf16[128,16,64]{0,2,1:T(8,128)(2,1)S(1)}, u32[]{:S(2)}, u32[]{:S(2)}) async-start(bf16[128,16,64]{0,2,1:T(8,128)(2,1)} %bitcast.20), calls=%async_computation.1 | async-start | bytes 524288 | tf_op jit(solution)/shard_map/all_to_all | solution.py:186
  195.7 4.7 copy-start.29
  195.7 46.9 %copy-start.7 = (bf16[2048,1,64]{0,2,1:T(8,128)(2,1)}, bf16[2048,1,64]{0,2,1:T(8,128)(2,1)S(1)}, u32[]{:S(2)}) copy-start(bf16[2048,1,64]{0,2,1:T(8,128)(2,1)S(1)} %get-tuple-element.529) | copy-start | bytes 786436
  195.7 46.9 %copy-start.10 = (bf16[2048,1,64]{0,2,1:T(8,128)(2,1)}, bf16[2048,1,64]{0,2,1:T(8,128)(2,1)S(1)}, u32[]{:S(2)}) copy-start(bf16[2048,1,64]{0,2,1:T(8,128)(2,1)S(1)} %get-tuple-element.548) | copy-start | bytes 786436
  195.7 4.7 copy-start.36
  195.7 31.0 %copy-start.40 = (bf16[1,2,128]{2,1,0:T(2,128)(2,1)S(1)}, bf16[1,2,128]{2,1,0:T(2,128)(2,1)}, u32[]{:S(2)}) copy-start(bf16[1,2,128]{2,1,0:T(2,128)(2,1)} %param.25) | copy-start | bytes 1540
  196.8 45.8 %all-to-all-start.3 = ((bf16[16,128,64]{1,2,0:T(8,128)(2,1)}), bf16[16,128,64]{1,2,0:T(8,128)(2,1)S(1)}, u32[]{:S(2)}, u32[]{:S(2)}) async-start(bf16[16,128,64]{1,2,0:T(8,128)(2,1)} %copy.76), calls=%async_computation.3 | async-start | bytes 524288 | tf_op jit(solution)/shard_map/all_to_all | solution.py:190
  272.6 109.6 %copy-start.4 = (f32[128,4096]{1,0:T(8,128)}, f32[128,4096]{1,0:T(8,128)S(1)}, u32[]{:S(2)}) copy-start(f32[128,4096]{1,0:T(8,128)S(1)} %fusion.43) | copy-start | bytes 6291460
  375.1 7.1 copy-start.3
  382.3 4.1 copy-start.20
  390.6 12.6 %all-to-all-start.4 = ((bf16[128,16,64]{0,2,1:T(8,128)(2,1)}), bf16[128,16,64]{0,2,1:T(8,128)(2,1)S(1)}, u32[]{:S(2)}, u32[]{:S(2)}) async-start(bf16[128,16,64]{0,2,1:T(8,128)(2,1)} %bitcast.36), calls=%async_computation.4 | async-start | bytes 524288 | tf_op jit(solution)/shard_map/all_to_all | solution.py:257
  396.0 153.2 %reduce-scatter.10.cloned.1.call-start = ((), (), s32[]{:S(2)}) async-start(), calls=%async_computation.14 | async-start | bytes 2359296 | tf_op jit(solution)/shard_map/reduce_scatter | solution.py:74
  399.3 4.9 copy-start.8
  399.3 4.9 copy-start.11
  410.2 6.2 copy-start
  416.9 4.7 copy-start.2
  429.1 6.3 copy-start
  435.9 4.9 copy-start.2
  448.4 6.2 copy-start
  455.1 4.9 copy-start.2
  467.5 6.2 copy-start
  474.3 4.9 copy-start.2
  480.7 17.9 %copy-start.32 = (bf16[4,512,64]{1,2,0:T(8,128)(2,1)S(1)}, bf16[4,512,64]{1,2,0:T(8,128)(2,1)}, u32[]{:S(2)}) copy-start(bf16[4,512,64]{1,2,0:T(8,128)(2,1)} %get-tuple-element.552) | copy-start | bytes 786436
  482.7 11.5 %all-to-all-start.6 = ((bf16[16,128,64]{1,2,0:T(8,128)(2,1)}), bf16[16,128,64]{1,2,0:T(8,128)(2,1)S(1)}, u32[]{:S(2)}, u32[]{:S(2)}) async-start(bf16[16,128,64]{1,2,0:T(8,128)(2,1)} %copy.81), calls=%async_computation.6 | async-start | bytes 524288 | tf_op jit(solution)/shard_map/all_to_all | solution.py:263
  494.2 26.9 %copy-start.31 = (bf16[16,128,64]{1,2,0:T(8,128)(2,1)}, bf16[16,128,64]{1,2,0:T(8,128)(2,1)S(1)}, u32[]{:S(2)}) copy-start(bf16[16,128,64]{1,2,0:T(8,128)(2,1)S(1)} %all-to-all-done.6) | copy-start | bytes 786436
  494.2 11.6 %all-to-all-start.7 = ((bf16[16,128,64]{1,2,0:T(8,128)(2,1)}), bf16[16,128,64]{1,2,0:T(8,128)(2,1)S(1)}, u32[]{:S(2)}, u32[]{:S(2)}) async-start(bf16[16,128,64]{1,2,0:T(8,128)(2,1)} %copy.82), calls=%async_computation.7 | async-start | bytes 524288 | tf_op jit(solution)/shard_map/all_to_all | solution.py:264
  498.5 117.6 %reduce-scatter.8.cloned.1.call-start = ((), (), s32[]{:S(2)}) async-start(), calls=%async_computation.13 | async-start | bytes 7077888 | tf_op jit(solution)/shard_map/reduce_scatter | solution.py:71
  505.8 15.3 %copy-start.23 = (bf16[16,128,64]{1,2,0:T(8,128)(2,1)}, bf16[16,128,64]{1,2,0:T(8,128)(2,1)S(1)}, u32[]{:S(2)}) copy-start(bf16[16,128,64]{1,2,0:T(8,128)(2,1)S(1)} %all-to-all-done.7) | copy-start | bytes 786436
  516.4 4.7 copy-start.25
  521.1 211.8 %reduce-scatter.12.cloned.1.call-start = ((), (), s32[]{:S(2)}) async-start(), calls=%async_computation.15 | async-start | bytes 9437184 | tf_op jit(solution)/shard_map/reduce_scatter | solution.py:71
  528.2 321.4 %reduce-scatter.14.cloned.1.call-start = ((), (), s32[]{:S(2)}) async-start(), calls=%async_computation.16 | async-start | bytes 9437184 | tf_op jit(solution)/shard_map/reduce_scatter | solution.py:74
  534.4 385.7 %reduce-scatter.16.cloned.1.call-start = ((), (), s32[]{:S(2)}) async-start(), calls=%async_computation.21 | async-start | bytes 294912
  534.5 5.9 copy-start.15
  534.5 5.9 copy-start.22
  534.5 5.9 copy-start.28
  540.3 6.2 copy-start.24
  546.8 302.8 %copy-start.41 = (u32[128]{0:T(128)S(1)}, u32[128]{0:T(128)}, u32[]{:S(2)}) copy-start(u32[128]{0:T(128)} %constant.81) | copy-start | bytes 1540
  549.1 503.6 %all-reduce.5.cloned.1.call-start = ((), (), s32[]{:S(2)}) async-start(), calls=%async_computation.22 | async-start | bytes 6291456 | tf_op jit(solution)/shard_map/psum | solution.py:82
  (32 other events, 66.0 us)
Sparse Core Ops, SparseCore 0:
  10.3 92.2 all-gather.14
  105.0 52.9 all-gather.16
  160.3 107.4 all-gather.18
  270.0 105.0 all-gather.20
  400.8 72.3 reduce-scatter.9
  521.3 94.8 reduce-scatter.7
  620.0 112.9 reduce-scatter.11
  737.3 112.2 reduce-scatter.13
  853.7 66.3 reduce-scatter.15
  922.7 129.9 all-reduce.4
where the time goes:
time: 1070 us
  waiting for transfers between devices  658 us (61%)
  blocking collectives  184 us (17%)
  matrix products  115 us (11%)
  starting transfers between devices  32.8 us (3%)
  local copies, waits for them, and re-layouts  30.6 us (3%)
  other arithmetic  16.4 us (2%)
  between operations  15.6 us (1%)
  loops' own time  13.6 us (1%)
    reduce_scatter x2, waiting for transfers between devices, reduce_terms(): lax.psum_scatter(terms[0].astype(jnp.bfloat16), 'fsdp', scatter_dimension...  184 us
    reduce_scatter x2, waiting for transfers between devices, reduce_terms(): lax.psum_scatter(terms[1].astype(jnp.bfloat16), 'fsdp', scatter_dimension...  117 us
    all_gather x1, waiting for transfers between devices, fetch_layer(): lax.all_gather(pieces[3], 'fsdp', axis=0, tiled=True)  103 us
    psum x1, waiting for transfers between devices, reduce_terms(): lax.psum(shares[0].astype(jnp.bfloat16), 'seq').astype(jnp.float32)  100 us
    unnamed x11, waiting for transfers between devices  55.4 us
    all_gather x1, waiting for transfers between devices, fetch_layer(): lax.all_gather(pieces[0], 'fsdp', axis=0, tiled=True)  45.1 us
    psum x1, blocking collectives, reduce_terms(): lax.psum(shares[2].astype(jnp.bfloat16), 'seq').astype(jnp.float32)  29.6 us
    all_gather x1, blocking collectives, fetch_layer(): lax.all_gather(pieces[7], 'fsdp', axis=0, tiled=True)  26.3 us
  transfers between devices with their start and end apart: 17, of which 13 were waited for; matrix products, arithmetic and copies ran while one was open for 12% of the time, Pallas kernels for 0%

commit v1 on v0

v1 whole, which is shorter than its diff:
```python
import functools

import jax
import jax.numpy as jnp
from jax import lax
from jax.experimental import pallas as pl
from jax.experimental.pallas import tpu as pltpu
from jax.sharding import PartitionSpec as P

NORM_EPS = 1e-06
NEG_FILL = -1e30
F32 = jnp.float32
BF16 = jnp.bfloat16
MESH = pl.DeviceIdType.MESH
NT = (((1,), (1,)), ((), ()))
TN = (((0,), (0,)), ((), ()))
NN = (((1,), (0,)), ((), ()))
VMEM_LIMIT = 60 * 1024 * 1024


def dot(left, right, dims=NN):
    return lax.dot_general(left, right, dims, preferred_element_type=F32)


class Place:
    def __init__(self):
        self.f = lax.axis_index("fsdp")
        self.s = lax.axis_index("seq")
        self.y = self.s // 4
        self.xl = (self.s // 2) % 2
        self.c = self.s % 2
        self.yp = (self.y + 1) % 4
        self.ym = (self.y + 3) % 4
        self.yo = (self.y + 2) % 4
        self.chip = self.s // 2
        self.j = self.y * 2 + self.c
        self.core = (self.f, self.slot(self.y, self.xl, 1 - self.c))
        self.xpart = (self.f, self.slot(self.y, 1 - self.xl, self.c))
        self.up = (self.f, self.slot(self.yp, self.xl, self.c))
        self.down = (self.f, self.slot(self.ym, self.xl, self.c))

    def slot(self, y, xl, c):
        return (y * 2 + xl) * 2 + c


def greet(me, seq=True, fsdp=True):
    barrier = pltpu.get_barrier_semaphore()
    count = 0
    if fsdp:
        for step in range(1, 8):
            pl.semaphore_signal(
                barrier, inc=1, device_id=((me.f + step) % 8, me.s), device_id_type=MESH
            )
        count += 7
    if seq:
        for step in range(1, 16):
            pl.semaphore_signal(
                barrier, inc=1, device_id=(me.f, (me.s + step) % 16), device_id_type=MESH
            )
        count += 15
    pl.semaphore_wait(barrier, count)


class Wire:
    def __init__(self, send_sem, recv_sem):
        self.send_sem, self.recv_sem = send_sem, recv_sem
        self.used = 0
        self.sent = []

    def send(self, src, dst, device):
        k = self.used
        self.used += 1
        copy = pltpu.make_async_remote_copy(
            src_ref=src,
            dst_ref=dst,
            send_sem=self.send_sem.at[k],
            recv_sem=self.recv_sem.at[k],
            device_id=device,
            device_id_type=MESH,
        )
        copy.start()
        self.sent.append(copy)
        return copy

    def drain(self):
        for copy in self.sent:
            copy.wait_send()
        self.sent = []


def to_fsdp(wire, me, src_of, dst_of):
    copies = []
    for step in range(1, 8):
        peer = (me.f + step) % 8
        copies.append(wire.send(src_of(peer), dst_of(me.f), (peer, me.s)))
    return copies


def arrived(copies):
    for copy in copies:
        copy.wait_recv()


class Gather8:
    def __init__(self, wire, me, ref):
        self.wire, self.me, self.ref = wire, me, ref
        self.half = ref.shape[1] // 2

    def slot(self, y, c=None):
        return y * 2 + (self.me.c if c is None else c)

    def start(self):
        w, me, r = self.wire, self.me, self.ref
        own = r.at[self.slot(me.y)]
        self.c_up = w.send(own, own, me.up)
        self.c_down = w.send(own, own, me.down)
        self.cores = [w.send(own, own, me.core)]

    def relay(self):
        w, me, r, h = self.wire, self.me, self.ref, self.half
        self.c_up.wait_recv()
        low = r.at[self.slot(me.ym)]
        head = r.at[self.slot(me.ym), pl.ds(0, h)]
        self.o_up = w.send(head, head, me.up)
        self.cores.append(w.send(low, low, me.core))
        self.c_down.wait_recv()
        high = r.at[self.slot(me.yp)]
        tail = r.at[self.slot(me.yp), pl.ds(h, h)]
        self.o_down = w.send(tail, tail, me.down)
        self.cores.append(w.send(high, high, me.core))

    def last(self):
        w, me, r = self.wire, self.me, self.ref
        self.o_up.wait_recv()
        self.o_down.wait_recv()
        far = r.at[self.slot(me.yo)]
        self.cores.append(w.send(far, far, me.core))

    def finish(self):
        arrived(self.cores)


class Gather16:
    def __init__(self, wire, me, ref):
        self.wire, self.me, self.ref = wire, me, ref
        self.half = ref.shape[1] // 2

    def slot(self, y, other=False):
        me = self.me
        return me.slot(y, 1 - me.xl if other else me.xl, me.c)

    def start(self):
        w, me, r = self.wire, self.me, self.ref
        own = r.at[self.slot(me.y)]
        self.cx = w.send(own, own, me.xpart)
        self.c_up = [w.send(own, own, me.up)]
        self.c_down = [w.send(own, own, me.down)]
        self.cores = [w.send(own, own, me.core)]

    def cross(self):
        w, me, r = self.wire, self.me, self.ref
        self.cx.wait_recv()
        part = r.at[self.slot(me.y, True)]
        self.c_up.append(w.send(part, part, me.up))
        self.c_down.append(w.send(part, part, me.down))
        self.cores.append(w.send(part, part, me.core))

    def relay(self, other):
        w, me, r, h = self.wire, self.me, self.ref, self.half
        self.c_up[int(other)].wait_recv()
        low = r.at[self.slot(me.ym, other)]
        head = r.at[self.slot(me.ym, other), pl.ds(0, h)]
        o_up = w.send(head, head, me.up)
        self.cores.append(w.send(low, low, me.core))
        self.c_down[int(other)].wait_recv()
        high = r.at[self.slot(me.yp, other)]
        tail = r.at[self.slot(me.yp, other), pl.ds(h, h)]
        o_down = w.send(tail, tail, me.down)
        self.cores.append(w.send(high, high, me.core))
        return o_up, o_down

    def last(self, pair, other):
        w, me, r = self.wire, self.me, self.ref
        arrived(pair)
        far = r.at[self.slot(me.yo, other)]
        self.cores.append(w.send(far, far, me.core))

    def run(self):
        self.cross()
        own = self.relay(False)
        part = self.relay(True)
        self.last(own, False)
        self.last(part, True)

    def finish(self):
        arrived(self.cores)


def full_row(params, row):
    return jnp.concatenate([params[f, row : row + 1, :] for f in range(8)], axis=1)


def norm_stats(values):
    mean_val = jnp.mean(values, axis=-1, keepdims=True)
    centered = values - mean_val
    variance = jnp.mean(centered * centered, axis=-1, keepdims=True)
    inverse = lax.rsqrt(variance + NORM_EPS)
    return centered * inverse, inverse


def head_half(me, rows128):
    return jnp.where(me.c == 0, rows128[:, :64], rows128[:, 64:])


def kernel_a(
    tok, gout, vin, pv, wq_in, wp_in, w1_in,
    nrm, grd, pv_all, wq_all, wp_all, w1_all, qa, ka, va, ow, at,
    v_all, om, ss, rs, as_, ar_,
):
    me = Place()
    wire = Wire(ss, rs)
    greet(me)
    pv_all[me.f] = pv[...]
    wq_all[me.f] = wq_in[...]
    wp_all[me.f] = wp_in[...]
    w1_all[me.f] = w1_in[...]
    v_all[me.s] = vin[...]
    got_pv = to_fsdp(wire, me, lambda p: pv, lambda f: pv_all.at[f])
    got_wq = to_fsdp(wire, me, lambda p: wq_in, lambda f: wq_all.at[f])
    normed, _ = norm_stats(tok[...].astype(F32))
    arrived(got_pv)
    params = pv_all[...].astype(F32)
    nrm[me.s] = (normed * full_row(params, 0) + full_row(params, 2)).astype(BF16)
    gather = Gather16(wire, me, nrm)
    gather.start()
    got_v = []
    for step in range(1, 16):
        peer = (me.s + step) % 16
        got_v.append(wire.send(vin, v_all.at[me.s], (me.f, peer)))
    grd[me.j] = (full_row(params, 9) * gout[...].astype(F32)).astype(BF16)
    gather.run()
    grad_gather = Gather8(wire, me, grd)
    grad_gather.start()
    half = pl.ds(pl.multiple_of(me.c * 64, 64), 64)
    got_wp = to_fsdp(wire, me, lambda p: wp_in.at[half], lambda f: wp_all.at[f, half])
    got_w1 = to_fsdp(wire, me, lambda p: w1_in, lambda f: w1_all.at[f])

    arrived(got_v)
    flags = v_all[:, 0, :].astype(F32)
    flags = jnp.concatenate([flags, jnp.zeros((112, 128), F32)], axis=0).T
    ext_lane = lax.broadcasted_iota(jnp.int32, (128, 64), 1)
    q_ext = jnp.where(ext_lane == 0, 1.0, 0.0).astype(BF16)
    v_ext = jnp.where(ext_lane < 3, 1.0, 0.0).astype(BF16)
    for blk in range(16):
        bias = (1.0 - flags[:, blk : blk + 1]) * NEG_FILL
        ext = jnp.where(ext_lane == 0, bias, jnp.where(ext_lane < 4, 1.0, 0.0))
        ka[blk * 128 : (blk + 1) * 128, 64:] = ext.astype(BF16)
    bias_rows = head_half(me, pv_all[me.s // 2].astype(F32))
    bias_q, bias_v = bias_rows[4:5, :], bias_rows[5:6, :]
    gather.finish()
    arrived(got_wq)
    wq = wq_all[...].reshape(1024, 256)

    def project(blk, carry):
        qkv = dot(nrm[blk], wq)
        rows = pl.ds(pl.multiple_of(blk * 128, 128), 128)
        query = ((qkv[:, :64] + bias_q).astype(BF16) * 0.125).astype(BF16)
        qa[rows, :] = jnp.concatenate([query, q_ext], axis=1)
        ka[rows, :64] = qkv[:, 64:128].astype(BF16)
        value = (qkv[:, 128:192] + bias_v).astype(BF16)
        va[rows, :] = jnp.concatenate([value, v_ext], axis=1)
        return carry

    lax.fori_loop(0, 16, project, 0)
    grad_gather.relay()

    def message(k, e):
        blk = ((me.chip + 1 + k) % 8) * 2 + e
        return pltpu.make_async_remote_copy(
            src_ref=om.at[blk],
            dst_ref=at.at[me.s],
            send_sem=as_.at[2 * k + e],
            recv_sem=ar_.at[2 * k + me.c],
            device_id=(me.f, blk),
            device_id_type=MESH,
        )

    out_lane = lax.broadcasted_iota(jnp.int32, (256, 128), 1)

    def attend(k):
        chip = (me.chip + 1 + k) % 8
        rows = pl.ds(pl.multiple_of(chip * 256, 256), 256)
        scores = dot(qa[rows, :], ka[...], NT)
        row_max = jnp.max(scores, axis=1, keepdims=True)
        terms = jnp.exp(scores - row_max).astype(BF16)
        mixed = dot(terms, va[...])
        total = mixed[:, 64:65]
        heads = mixed / total
        log_sum = row_max + jnp.log(total)
        ow[rows, :] = jnp.where(out_lane < 64, heads, log_sum)
        rounded = heads[:, :64].astype(BF16)
        for e in range(2):
            piece = rounded[e * 128 : (e + 1) * 128]
            om[chip * 2 + e] = jnp.concatenate([piece[:64], piece[64:]], axis=1)

    def step(k, carry):
        attend(k)
        message(k, 0).start()
        message(k, 1).start()
        return carry

    lax.fori_loop(0, 4, step, 0)
    grad_gather.last()
    lax.fori_loop(4, 7, step, 0)
    attend(7)
    at[me.s] = om[me.s]
    partner = wire.send(om.at[me.s + 1 - 2 * me.c], at.at[me.s], me.core)

    def collect(k, carry):
        for e in range(2):
            copy = message(k, e)
            copy.wait_send()
            src = ((me.chip + 7 - k) % 8) * 2 + e
            pltpu.make_async_remote_copy(
                src_ref=om.at[src],
                dst_ref=at.at[src],
                send_sem=as_.at[2 * k + e],
                recv_sem=ar_.at[2 * k + e],
                device_id=(me.f, src),
                device_id_type=MESH,
            ).wait_recv()
        return carry

    lax.fori_loop(0, 7, collect, 0)
    partner.wait_recv()
    arrived(got_wp)
    swap = []
    for f in range(8):
        swap.append(wire.send(wp_all.at[f, half], wp_all.at[f, half], me.core))
    grad_gather.finish()
    arrived(got_w1)
    arrived(swap)
    wire.drain()


def vmem(count):
    return [pl.BlockSpec(memory_space=pltpu.VMEM)] * count


def sds(shape, dtype):
    return jax.ShapeDtypeStruct(shape, dtype)


def call_a(*args):
    outs = (
        sds((16, 128, 1024), BF16),
        sds((8, 128, 1024), BF16),
        sds((8, 16, 128), BF16),
        sds((8, 128, 256), BF16),
        sds((8, 128, 1024), BF16),
        sds((8, 128, 512), BF16),
        sds((2048, 128), BF16),
        sds((2048, 128), BF16),
        sds((2048, 128), BF16),
        sds((2048, 128), F32),
        sds((16, 64, 128), BF16),
    )
    return pl.pallas_call(
        kernel_a,
        out_shape=outs,
        in_specs=vmem(len(args)),
        out_specs=vmem(len(outs)),
        scratch_shapes=[
            pltpu.VMEM((16, 16, 128), BF16),
            pltpu.VMEM((16, 64, 128), BF16),
            pltpu.SemaphoreType.DMA((96,)),
            pltpu.SemaphoreType.DMA((96,)),
            pltpu.SemaphoreType.DMA((14,)),
            pltpu.SemaphoreType.DMA((14,)),
        ],
        name="front",
        compiler_params=pltpu.CompilerParams(
            collective_id=1, has_side_effects=True, vmem_limit_bytes=VMEM_LIMIT
        ),
    )(*args)


class ReduceY:
    def __init__(self, wire, me, part, slot, from_core, from_far, from_near):
        self.wire, self.me, self.part, self.slot = wire, me, part, slot
        self.from_core, self.from_far, self.from_near = from_core, from_far, from_near
        self.order = (me.yo, me.yp, me.ym, me.y)

    def start(self):
        me = self.me
        self.cores = []
        for d, y in enumerate(self.order):
            src = self.part.at[self.slot(y, 1 - me.c)]
            self.cores.append(self.wire.send(src, self.from_core.at[d], me.core))

    def combine(self, d):
        self.cores[d].wait_recv()
        own = self.part[self.slot(self.order[d], self.me.c)]
        total = own.astype(F32) + self.from_core[d].astype(F32)
        self.from_core[d] = total.astype(BF16)

    def far(self):
        w, me, acc = self.wire, self.me, self.from_core
        h = acc.shape[1] // 2
        self.head, self.tail = pl.ds(0, h), pl.ds(h, h)
        self.combine(0)
        self.f_up = w.send(acc.at[0, self.head], self.from_far.at[0], me.up)
        self.f_down = w.send(acc.at[0, self.tail], self.from_far.at[1], me.down)
        self.combine(1)
        self.n_up = [w.send(acc.at[1, self.tail], self.from_near.at[0, self.tail], me.up)]
        self.combine(2)
        self.n_down = [w.send(acc.at[2, self.head], self.from_near.at[1, self.head], me.down)]

    def near(self):
        w, me, acc = self.wire, self.me, self.from_core
        self.f_up.wait_recv()
        total = acc[1, self.head].astype(F32) + self.from_far[0].astype(F32)
        acc[1, self.head] = total.astype(BF16)
        self.n_up.append(w.send(acc.at[1, self.head], self.from_near.at[0, self.head], me.up))
        self.f_down.wait_recv()
        total = acc[2, self.tail].astype(F32) + self.from_far[1].astype(F32)
        acc[2, self.tail] = total.astype(BF16)
        self.n_down.append(w.send(acc.at[2, self.tail], self.from_near.at[1, self.tail], me.down))

    def result(self):
        self.cores[3].wait_recv()
        own = self.part[self.slot(self.me.y, self.me.c)]
        total = own.astype(F32) + self.from_core[3].astype(F32)
        arrived(self.n_up)
        arrived(self.n_down)
        return total + self.from_near[0].astype(F32) + self.from_near[1].astype(F32)


def norm_back(cotangent, gain, normed, inverse):
    scaled = cotangent * gain
    first = jnp.mean(scaled, axis=-1, keepdims=True)
    second = jnp.mean(scaled * normed, axis=-1, keepdims=True)
    return inverse * (scaled - first - normed * second)


def column_sum(values):
    return jnp.sum(values, axis=0, keepdims=True)


def kernel_b(
    tok, gout, pv_all, at, wp_in, w1_in, w2_in, grd,
    mid, gmid, atg, mp, dw1, dw2, gh, gac, vec, db1,
    w2_all, nmg, act, gpre, gn, r_core, r_far, r_near, msg, gat, ss, rs,
):
    me = Place()
    wire = Wire(ss, rs)
    greet(me)
    mine = pl.ds(pl.multiple_of(me.j * 64, 64), 64)
    w2_all[me.f] = w2_in[mine]
    got_w2 = to_fsdp(wire, me, lambda p: w2_in.at[mine], lambda f: w2_all.at[f])
    params = pv_all[...].astype(F32)
    heads = [jnp.concatenate([at[h, :, :64], at[h, :, 64:]], axis=0) for h in range(16)]
    attn_tok = jnp.concatenate(heads, axis=1)
    atg[me.j] = attn_tok
    wp = wp_in[...].reshape(1024, 1024)
    branch = dot(attn_tok, wp) + full_row(params, 6)
    middle = tok[...].astype(F32) + full_row(params, 8) * branch
    mid[...] = middle
    normed, inverse = norm_stats(middle)
    gain = full_row(params, 1)
    nmg[me.j] = (normed * gain + full_row(params, 3)).astype(BF16)
    gather = Gather8(wire, me, nmg)
    gather.start()
    gather.relay()
    attn_gather = Gather8(wire, me, atg)
    attn_gather.start()
    gather.last()
    gather.finish()
    arrived(got_w2)
    bias_one = jnp.concatenate([params[f, 10:11, :64] for f in range(8)], axis=1)

    def feed(b, carry):
        two = pl.ds(2 * b, 2)
        rows = pl.ds(pl.multiple_of(b * 256, 256), 256)
        w1 = w1_in[...].reshape(1024, 512)
        w2 = w2_all[...].reshape(512, 1024)
        pre = dot(nmg[two].reshape(256, 1024), w1) + bias_one
        cdf = 0.5 * (1.0 + lax.erf(pre * 0.7071067811865476))
        acts = (pre * cdf).astype(BF16)
        act[rows, :] = acts
        mp[two] = dot(acts, w2).astype(BF16).reshape(2, 128, 1024)
        grad_act = dot(grd[two].reshape(256, 1024), w2, NT)
        slope = cdf + pre * jnp.exp(-0.5 * pre * pre) * 0.3989422804014327
        grad_pre = (grad_act * slope).astype(BF16)
        gpre[rows, :] = grad_pre
        gn[two] = dot(grad_pre, w1, NT).astype(BF16).reshape(2, 128, 1024)
        return carry + column_sum(grad_pre.astype(F32))

    attn_gather.relay()
    db1[...] = lax.fori_loop(0, 4, feed, jnp.zeros((1, 512), F32))
    slot = lambda y, c: y * 2 + c
    reduce = ReduceY(wire, me, gn, slot, r_core, r_far, r_near)
    reduce.start()
    reduce.far()
    attn_gather.last()
    dw2[...] = dot(act[...], grd[...].reshape(1024, 1024), TN).astype(BF16).reshape(8, 64, 1024)
    reduce.near()
    dw1[...] = dot(nmg[...].reshape(1024, 1024), gpre[...], TN).astype(BF16).reshape(8, 128, 512)
    cotangent = reduce.result()
    grad_middle = gout[...].astype(F32) + norm_back(cotangent, gain, normed, inverse)
    gmid[...] = grad_middle
    grad_attn = (full_row(params, 8) * grad_middle).astype(BF16)
    gat[...] = grad_attn
    grad_tok = dot(grad_attn, wp, NT).astype(BF16)
    for h in range(16):
        piece = grad_tok[:, h * 64 : (h + 1) * 64]
        msg[h] = jnp.concatenate([piece[:64], piece[64:]], axis=1)
    gh[me.s] = msg[me.s]
    copies = []
    for step in range(1, 16):
        peer = (me.s + step) % 16
        copies.append(wire.send(msg.at[peer], gh.at[me.s], (me.f, peer)))
    for step in range(1, 8):
        peer = (me.j + step) % 8
        cols = pl.ds(pl.multiple_of(peer * 128, 128), 128)
        device = (me.f, me.slot(peer // 2, me.xl, peer % 2))
        copies.append(wire.send(gat.at[:, cols], gac.at[me.j], device))
    gac[me.j] = gat[:, pl.ds(pl.multiple_of(me.j * 128, 128), 128)]
    zero = jnp.zeros((1, 1024), F32)
    rows = [
        zero,
        column_sum(cotangent * normed),
        zero,
        column_sum(cotangent),
        zero,
        zero,
        column_sum(grad_attn.astype(F32)),
        column_sum(grd[me.j].astype(F32)),
        column_sum(grad_middle * branch),
        jnp.zeros((7, 1024), F32),
    ]
    vec[...] = jnp.concatenate(rows, axis=0)
    attn_gather.finish()
    arrived(copies)
    wire.drain()


def call_b(*args):
    outs = (
        sds((128, 1024), F32),
        sds((128, 1024), F32),
        sds((8, 128, 1024), BF16),
        sds((8, 128, 1024), BF16),
        sds((8, 128, 512), BF16),
        sds((8, 64, 1024), BF16),
        sds((16, 64, 128), BF16),
        sds((8, 128, 128), BF16),
        sds((16, 1024), F32),
        sds((1, 512), F32),
    )
    return pl.pallas_call(
        kernel_b,
        out_shape=outs,
        in_specs=vmem(len(args)),
        out_specs=vmem(len(outs)),
        scratch_shapes=[
            pltpu.VMEM((8, 64, 1024), BF16),
            pltpu.VMEM((8, 128, 1024), BF16),
            pltpu.VMEM((1024, 512), BF16),
            pltpu.VMEM((1024, 512), BF16),
            pltpu.VMEM((8, 128, 1024), BF16),
            pltpu.VMEM((4, 128, 1024), BF16),
            pltpu.VMEM((2, 64, 1024), BF16),
            pltpu.VMEM((2, 128, 1024), BF16),
            pltpu.VMEM((16, 64, 128), BF16),
            pltpu.VMEM((128, 1024), BF16),
            pltpu.SemaphoreType.DMA((96,)),
            pltpu.SemaphoreType.DMA((96,)),
        ],
        name="middle",
        compiler_params=pltpu.CompilerParams(
            collective_id=2, has_side_effects=True, vmem_limit_bytes=VMEM_LIMIT
        ),
    )(*args)


def three_parts(values):
    first = values.astype(BF16)
    rest = values - first.astype(F32)
    second = rest.astype(BF16)
    third = (rest - second.astype(F32)).astype(BF16)
    return first, second, third


def kernel_c(
    tok, gout, pv_all, wq_all, nrm, qa, ka, va, ow, gh, mid, gmid, atg, mp, dw1, dw2, gac, vecb, db1,
    res, gtok, o_qkv, o_proj, o_fc1, o_fc2, o_vec,
    ga, qb, kt, dk, dv, dq, pn, m_core, m_far, m_near,
    c_own, f_own, n_own, c_oth, f_oth, n_oth, x_sum, x_in,
    dwp, r1, r2, rp, x1, x2, xp, g1, g2, gp, dwq, rq, gq, vs, vr, vq, ss, rs,
):
    me = Place()
    wire = Wire(ss, rs)
    greet(me)
    params = pv_all[...].astype(F32)
    slot = lambda y, c: y * 2 + c
    mlp = ReduceY(wire, me, mp, slot, m_core, m_far, m_near)
    mlp.start()
    got = to_fsdp(wire, me, lambda p: dw1.at[p], lambda f: r1.at[f])
    got += to_fsdp(wire, me, lambda p: dw2.at[p], lambda f: r2.at[f])
    proj_cols = gac[...].reshape(1024, 128)
    dwp[...] = dot(atg[...].reshape(1024, 1024), proj_cols, TN).astype(BF16).reshape(8, 128, 128)
    got += to_fsdp(wire, me, lambda p: dwp.at[p], lambda f: rp.at[f])
    r1[me.f] = dw1[me.f]
    r2[me.f] = dw2[me.f]
    rp[me.f] = dwp[me.f]

    lane = lax.broadcasted_iota(jnp.int32, (128, 128), 1)
    for blk in range(16):
        rows = slice(blk * 128, (blk + 1) * 128)
        packed = gh[blk]
        grad = jnp.concatenate([packed[:, :64], packed[:, 64:]], axis=0)
        heads = ow[rows, :]
        delta = jnp.sum(grad.astype(F32) * heads[:, :64], axis=1, keepdims=True)
        d1, d2, d3 = three_parts(-delta)
        l1, l2, l3 = three_parts(-heads[:, 64:65])
        wide = jnp.concatenate([grad, jnp.zeros((128, 64), BF16)], axis=1).astype(F32)
        wide = jnp.where(lane == 64, d1.astype(F32), wide)
        wide = jnp.where(lane == 65, d2.astype(F32), wide)
        wide = jnp.where(lane == 66, d3.astype(F32), wide)
        ga[rows, :] = wide.astype(BF16)
        wide = qa[rows, :].astype(F32)
        wide = jnp.where(lane == 65, l1.astype(F32), wide)
        wide = jnp.where(lane == 66, l2.astype(F32), wide)
        wide = jnp.where(lane == 67, l3.astype(F32), wide)
        qb[rows, :] = wide.astype(BF16)
        kt[:, rows] = ka[rows, :].astype(F32).T.astype(BF16)
    dk[...] = jnp.zeros_like(dk)
    dv[...] = jnp.zeros_like(dv)
    mlp.far()

    def back(b, carry):
        rows = pl.ds(pl.multiple_of(b * 256, 256), 256)
        query, grad = qb[rows, :], ga[rows, :]
        probs = jnp.exp(dot(ka[...], query, NT))
        dv[...] += dot(probs.astype(BF16), grad)
        slope = dot(va[...], grad, NT)
        scores = (probs * slope).astype(BF16)
        dk[...] += dot(scores, query)
        turned = dot(kt[...], scores)
        dq[rows, :64] = (turned.T[:, :64] * 0.125).astype(BF16)
        return carry

    lax.fori_loop(0, 4, back, 0)
    mlp.near()
    lax.fori_loop(4, 8, back, 0)
    dq[:, 64:128] = dk[:, :64].astype(BF16)
    dq[:, 128:] = jnp.concatenate(
        [dv[:, :64].astype(BF16), jnp.zeros((2048, 64), BF16)], axis=1
    )

    def spread(blk, carry):
        rows = pl.ds(pl.multiple_of(blk * 128, 128), 128)
        wq = wq_all[...].reshape(1024, 256)
        pn[blk] = dot(dq[rows, :], wq, NT).astype(BF16)
        return carry

    lax.fori_loop(0, 16, spread, 0)
    others = ReduceY(
        wire, me, pn, lambda y, c: me.slot(y, 1 - me.xl, c), c_oth, f_oth, n_oth
    )
    owns = ReduceY(wire, me, pn, lambda y, c: me.slot(y, me.xl, c), c_own, f_own, n_own)
    others.start()
    owns.start()
    others.far()
    owns.far()

    grad_wq = dot(nrm[...].reshape(2048, 1024), dq[...], TN)
    dwq[...] = grad_wq.astype(BF16).reshape(8, 128, 256)
    rq[me.f] = dwq[me.f]
    got_q = to_fsdp(wire, me, lambda p: dwq.at[p], lambda f: rq.at[f])

    sums = column_sum(dq[...].astype(F32))
    mlp_out = mlp.result() + full_row(params, 7)
    res[...] = (mid[...] + full_row(params, 9) * mlp_out).astype(BF16)
    grad_scale = column_sum(gout[...].astype(F32) * mlp_out)
    vec = vecb[...]
    head_at = me.s // 2
    zero64 = jnp.zeros((1, 64), F32)
    for f in range(8):
        w_blk = wq_all[f].astype(F32)
        first = jnp.sum(w_blk * grad_wq[f * 128 : (f + 1) * 128], axis=1, keepdims=True)
        second = jnp.sum(w_blk * sums, axis=1, keepdims=True)
        turned = jnp.where(lane == 0, first, jnp.where(lane == 1, second, 0.0)).T
        total = turned[1:2]
        gain = (turned[0:1] - params[f, 2:3] * total) / params[f, 0:1]
        cols = slice(f * 128, (f + 1) * 128)
        placed = []
        for part in (sums[:, :64], sums[:, 128:192]):
            pair = jnp.where(
                me.c == 0,
                jnp.concatenate([part, zero64], axis=1),
                jnp.concatenate([zero64, part], axis=1),
            )
            placed.append(jnp.where(head_at == f, pair, 0.0))
        piece = db1[:, f * 64 : (f + 1) * 64]
        pair = jnp.where(
            me.c == 0,
            jnp.concatenate([piece, zero64], axis=1),
            jnp.concatenate([zero64, piece], axis=1),
        )
        bias = [jnp.where(me.y == row, pair, 0.0) for row in range(4)]
        vs[f] = jnp.concatenate(
            [
                gain,
                vec[1:2, cols],
                total,
                vec[3:4, cols],
                placed[0],
                placed[1],
                vec[6:9, cols],
                grad_scale[:, cols],
                *bias,
                jnp.zeros((2, 128), F32),
            ],
            axis=0,
        )
    vr[me.f] = vs[me.f]
    got_v = to_fsdp(wire, me, lambda p: vs.at[p], lambda f: vr.at[f])
    others.near()
    owns.near()

    arrived(got)

    def eight(ref):
        total = ref[0].astype(F32)
        for f in range(1, 8):
            total = total + ref[f].astype(F32)
        return total.astype(BF16)

    x1[0] = eight(r1)
    x2[0] = eight(r2)
    xp[0] = eight(rp)
    swap = [wire.send(x.at[0], x.at[1], me.xpart) for x in (x1, x2, xp)]

    x_sum[...] = others.result().astype(BF16)
    crossed = wire.send(x_sum, x_in, me.xpart)

    arrived(got_q)
    gq[me.s] = eight(rq)
    gather_q = Gather16(wire, me, gq)
    gather_q.start()
    arrived(got_v)
    total = vr[0]
    for f in range(1, 8):
        total = total + vr[f]
    vq[me.s] = total
    got_vq = []
    for step in range(1, 16):
        got_vq.append(wire.send(vq.at[me.s], vq.at[me.s], (me.f, (me.s + step) % 16)))

    arrived(swap)
    gathers = []
    for x, g in ((x1, g1), (x2, g2), (xp, gp)):
        g[me.j] = (x[0].astype(F32) + x[1].astype(F32)).astype(BF16)
        gathers.append(Gather8(wire, me, g))
    for gather in gathers:
        gather.start()
    cotangent = owns.result()
    gather_q.run()
    for gather in gathers:
        gather.relay()
    normed, inverse = norm_stats(tok[...].astype(F32))
    crossed.wait_recv()
    cotangent = cotangent + x_in[...].astype(F32)
    gtok[...] = gmid[...] + norm_back(cotangent, full_row(params, 0), normed, inverse)
    for gather in gathers:
        gather.last()
    gather_q.finish()
    for part in range(3):
        cols = slice(part * 64, (part + 1) * 64)
        for k in range(8):
            pair = jnp.concatenate([gq[2 * k, :, cols], gq[2 * k + 1, :, cols]], axis=1)
            o_qkv[:, part * 1024 + k * 128 : part * 1024 + (k + 1) * 128] = pair.astype(F32)
    for gather in gathers:
        gather.finish()
    for j in range(8):
        o_proj[:, j * 128 : (j + 1) * 128] = gp[j].astype(F32)
        o_fc2[j] = g2[j].astype(F32)
    for f in range(8):
        cols = slice(f * 64, (f + 1) * 64)
        for k in range(4):
            pair = jnp.concatenate([g1[2 * k, :, cols], g1[2 * k + 1, :, cols]], axis=1)
            o_fc1[:, f * 512 + k * 128 : f * 512 + (k + 1) * 128] = pair.astype(F32)
    arrived(got_vq)
    total = vq[0]
    for s in range(1, 16):
        total = total + vq[s]
    o_vec[...] = total
    wire.drain()


def call_c(*args):
    outs = (
        sds((128, 1024), BF16),
        sds((128, 1024), F32),
        sds((128, 3072), F32),
        sds((128, 1024), F32),
        sds((128, 4096), F32),
        sds((8, 64, 1024), F32),
        sds((16, 128), F32),
    )
    block = (128, 1024)
    reduce = [
        pltpu.VMEM((4, *block), BF16),
        pltpu.VMEM((2, 64, 1024), BF16),
        pltpu.VMEM((2, *block), BF16),
    ]
    return pl.pallas_call(
        kernel_c,
        out_shape=outs,
        in_specs=vmem(len(args)),
        out_specs=vmem(len(outs)),
        scratch_shapes=[
            pltpu.VMEM((2048, 128), BF16),
            pltpu.VMEM((2048, 128), BF16),
            pltpu.VMEM((128, 2048), BF16),
            pltpu.VMEM((2048, 128), F32),
            pltpu.VMEM((2048, 128), F32),
            pltpu.VMEM((2048, 256), BF16),
            pltpu.VMEM((16, *block), BF16),
            *reduce,
            *reduce,
            *reduce,
            pltpu.VMEM(block, BF16),
            pltpu.VMEM(block, BF16),
            pltpu.VMEM((8, 128, 128), BF16),
            pltpu.VMEM((8, 128, 512), BF16),
            pltpu.VMEM((8, 64, 1024), BF16),
            pltpu.VMEM((8, 128, 128), BF16),
            pltpu.VMEM((2, 128, 512), BF16),
            pltpu.VMEM((2, 64, 1024), BF16),
            pltpu.VMEM((2, 128, 128), BF16),
            pltpu.VMEM((8, 128, 512), BF16),
            pltpu.VMEM((8, 64, 1024), BF16),
            pltpu.VMEM((8, 128, 128), BF16),
            pltpu.VMEM((8, 128, 256), BF16),
            pltpu.VMEM((8, 128, 256), BF16),
            pltpu.VMEM((16, 128, 256), BF16),
            pltpu.VMEM((8, 16, 128), F32),
            pltpu.VMEM((8, 16, 128), F32),
            pltpu.VMEM((16, 16, 128), F32),
            pltpu.SemaphoreType.DMA((192,)),
            pltpu.SemaphoreType.DMA((192,)),
        ],
        name="back",
        compiler_params=pltpu.CompilerParams(
            collective_id=3, has_side_effects=True, vmem_limit_bytes=VMEM_LIMIT
        ),
    )(*args)


def pick_params(norm_gain, shifts, layer_scale, fc1_bias, j):
    bias = lax.dynamic_index_in_dim(fc1_bias[0].reshape(8, 64), j, 0)
    bias = jnp.pad(bias, ((0, 0), (0, 64)))
    return jnp.concatenate(
        [norm_gain[0], shifts[0], layer_scale[0], bias, jnp.zeros((5, 128), BF16)], axis=0
    )


def body(
    tokens, image_ids, valid, w_qkv, w_proj, w_fc1, w_fc2,
    norm_gain, shifts, layer_scale, fc1_bias, grad_out,
):
    s = lax.axis_index("seq")
    j = (s // 4) * 2 + s % 2
    pv = pick_params(norm_gain, shifts, layer_scale, fc1_bias, j)
    vin = jnp.broadcast_to(valid.astype(BF16)[None, :], (16, 128))
    wq = lax.dynamic_index_in_dim(w_qkv[0].reshape(128, 3, 16, 64), s, 2, keepdims=False)
    wq = jnp.pad(wq.reshape(128, 192), ((0, 0), (0, 64)))
    w1 = lax.dynamic_index_in_dim(w_fc1[0].reshape(128, 8, 8, 64), j, 2, keepdims=False)
    w1 = w1.reshape(128, 512)
    nrm, grd, pv_all, wq_all, wp_all, w1_all, qa, ka, va, ow, at = call_a(
        tokens, grad_out, vin, pv, wq, w_proj[0], w1
    )
    mid, gmid, atg, mp, dw1, dw2, gh, gac, vec, db1 = call_b(
        tokens, grad_out, pv_all, at, wp_all, w1_all, w_fc2[0], grd
    )
    res, gtok, g_qkv, g_proj, g_fc1, g_fc2, g_vec = call_c(
        tokens, grad_out, pv_all, wq_all, nrm, qa, ka, va, ow, gh,
        mid, gmid, atg, mp, dw1, dw2, gac, vec, db1,
    )
    return (
        res,
        gtok,
        g_qkv[None],
        g_proj[None],
        g_fc1[None],
        g_fc2.reshape(1, 512, 1024),
        g_vec[None, 0:2],
        g_vec[None, 2:8],
        g_vec[None, 8:10],
        g_vec[10:14].reshape(1, 512),
    )


def solution(mesh):
    rows = P(("fsdp", "seq"), None)
    flat = P(("fsdp", "seq"))
    mats = P(None, "fsdp", None)
    vecs = P(None, None, "fsdp")
    bias = P(None, "fsdp")
    return jax.shard_map(
        body,
        mesh=mesh,
        in_specs=(rows, flat, flat, mats, mats, mats, mats, vecs, vecs, vecs, bias, rows),
        out_specs=(rows, rows, mats, mats, mats, mats, vecs, vecs, vecs, bias),
        check_vma=False,
    )
```

time: 1070 us -> 229 us (0.21)
  waiting for transfers between devices: 658 us -> 0 us
  Pallas kernels: 0 us -> 206 us
  blocking collectives: 184 us -> 0 us
  matrix products: 115 us -> 0 us
  starting transfers between devices: 32.8 us -> 0 us
  other arithmetic: 16.4 us -> 1.44 us
  between operations: 15.6 us -> 0.76 us
  loops' own time: 13.6 us -> 0 us
    reduce_scatter x4 -> x0, waiting for transfers between devices: 300 us -> none  [the longest x2 184 us: reduce_terms(): lax.psum_scatter(terms[0].astype(jnp.bfloat16), 'fsdp', scatter_dimension...]
    pallas_call x0 -> x3, Pallas kernels: none -> 206 us  [the longest x1 77.4 us: call_c(): pl.pallas_call(kernel_c, out_shape=outs, in_specs=vmem(len(args)), out_sp...]
    all_gather x4 -> x0, waiting for transfers between devices: 170 us -> none  [the longest x1 103 us: fetch_layer(): lax.all_gather(pieces[3], 'fsdp', axis=0, tiled=True)]
    all_gather x6 -> x0, blocking collectives: 128 us -> none  [the longest x1 26.3 us: fetch_layer(): lax.all_gather(pieces[7], 'fsdp', axis=0, tiled=True)]
    dot_general x40 -> x0, matrix products: 115 us -> none  [the longest x8 22 us: block_scores(): jnp.einsum('qhd,khd->hqk', query_blk, key_h, preferred_element_type=jnp.f...]
    psum x1 -> x0, waiting for transfers between devices: 100 us -> none  [reduce_terms(): lax.psum(shares[0].astype(jnp.bfloat16), 'seq').astype(jnp.float32)]
    unnamed x11 -> x0, waiting for transfers between devices: 55.4 us -> none
    all_to_all x7 -> x0, starting transfers between devices: 32 us -> none  [the longest x1 5.39 us: backward_layer(): lax.all_to_all(grad_attn_tok, 'seq', split_axis=1, concat_axis=0, tiled=T...]
  transfers between devices with their start and end apart: 17 -> 0, of which waited for: 13 -> 0; matrix products, arithmetic and copies ran while one was open for 12% -> 0% of each run, Pallas kernels for 0% -> 0%
where the time goes in v1:
time: 229 us
  Pallas kernels  206 us (90%)
  local copies, waits for them, and re-layouts  20.4 us (9%)
    pallas_call x1, Pallas kernels, call_c(): pl.pallas_call(kernel_c, out_shape=outs, in_specs=vmem(len(args)), out_sp...  77.4 us
    pallas_call x1, Pallas kernels, call_a(): pl.pallas_call(kernel_a, out_shape=outs, in_specs=vmem(len(args)), out_sp...  70.7 us
    pallas_call x1, Pallas kernels, call_b(): pl.pallas_call(kernel_b, out_shape=outs, in_specs=vmem(len(args)), out_sp...  57.8 us
    unnamed x19, local copies, waits for them, and re-layouts  12.3 us

profile of v1, /device:TPU:1, one launch (start us, length us, event | category | flops | bytes accessed | tf_op | source)
XLA Modules:
  0.0 228.5 jit_solution(7726335160913772664)
XLA Ops:
  0.6 0.0 copy-start.3
  0.7 0.7 convert_element_type.7
  1.4 0.7 reduce
  2.1 0.1 reshape_squeeze.9
  2.2 2.5 %concatenate.3.pv = bf16[16,128]{1,0:T(8,128)(2,1)} concatenate(bf16[2,128]{1,0:T(2,128)(2,1)} %bitcast.32, bf16[6,128]{1,0:T(8,128)(2,1)} %bitcast.30, bf16[2,128]{1,0:T(2,128)(2,1)} %bitcast.33, bf16[1,128]{1,0:T(2,128)(2,1)S(1)} %pad.8, bf16[5,128]{1,0:T(8,128)(2,1)S(1)} %broadcast_in_dim.28), dimensions={0} | concatenate | bytes 8192 | tf_op jit(solution)/shard_map/concatenate | solution.py:866
  4.8 0.6 broadcast_in_dim.27.vin
  5.4 1.5 copy.24
  6.9 0.1 copy.25
  7.0 0.6 pad.9.wq_in
  7.7 0.0 copy-done.3
  7.7 0.7 copy.26
  8.3 0.8 copy.27.w1_in
  9.1 70.7 %front.1 = (bf16[16,128,1024]{2,1,0:T(8,128)(2,1)}, bf16[8,128,1024]{2,1,0:T(8,128)(2,1)}, bf16[8,16,128]{2,1,0:T(8,128)(2,1)}, bf16[8,128,256]{2,1,0:T(8,128)(2...) custom-call(bf16[128,1024]{1,0:T(8,128)(2,1)} %tok.5, ...), custom_call_target="tpu_custom_call" | custom-call | tf_op jit(solution)/shard_map/front/pallas_call | solution.py:368
  79.9 57.8 %middle.1 = (f32[128,1024]{1,0:T(8,128)}, f32[128,1024]{1,0:T(8,128)}, bf16[8,128,1024]{2,1,0:T(8,128)(2,1)}, bf16[8,128,1024]{2,1,0:T(8,128)(2,1)}, bf16[8,128,...) custom-call(bf16[128,1024]{1,0:T(8,128)(2,1)} %tok.5, ...), custom_call_target="tpu_custom_call" | custom-call | tf_op jit(solution)/shard_map/middle/pallas_call | solution.py:561
  137.7 77.4 %back.1 = (bf16[128,1024]{1,0:T(8,128)(2,1)}, f32[128,1024]{1,0:T(8,128)}, f32[128,3072]{1,0:T(8,128)}, f32[128,1024]{1,0:T(8,128)}, f32[128,4096]{1,0:T(8,128)}...) custom-call(bf16[128,1024]{1,0:T(8,128)(2,1)} %tok.5, bf16[128,1024]{1,0:T(8,128)(2,1)} %gout.5, ...), custom_call_target="tpu_custom_call" | custom-call | tf_op jit(solution)/shard_map/back/pallas_call | solution.py:819
  215.1 0.0 copy-start.2
  215.1 1.4 slice.15
  216.4 1.3 slice_bitcast_fusion.1
  217.7 0.7 slice_bitcast_fusion
  218.4 0.6 copy.28
  219.0 1.7 copy.35
  220.6 0.0 copy-start.4
  220.6 1.9 copy.36
  222.6 0.0 copy-done.2
  222.6 0.0 copy-start.1
  222.6 1.1 copy.37
  223.7 0.0 copy-done.4
  223.7 0.8 copy.38
  224.5 0.3 copy-done.1
  224.8 0.0 copy-start
  224.8 1.3 copy.39
  226.2 1.0 copy-done
  227.2 1.3 copy.40
  (5 shorter events, 0.1 us)
Async XLA Ops:
  0.6 7.0 %copy-start.3 = (bf16[1,128,4096]{2,1,0:T(8,128)(2,1)S(1)}, bf16[1,128,4096]{2,1,0:T(8,128)(2,1)}, u32[]{:S(2)}) copy-start(bf16[1,128,4096]{2,1,0:T(8,128)(2,1)} %param.16) | copy-start | bytes 3145732
  215.1 7.5 %copy-start.2 = (f32[128,3072]{1,0:T(8,128)S(1)}, f32[128,3072]{1,0:T(8,128)}, u32[]{:S(2)}) copy-start(f32[128,3072]{1,0:T(8,128)} %get-tuple-element.61) | copy-start | bytes 4718596
  220.6 3.1 %copy-start.4 = (f32[128,1024]{1,0:T(8,128)S(1)}, f32[128,1024]{1,0:T(8,128)}, u32[]{:S(2)}) copy-start(f32[128,1024]{1,0:T(8,128)} %get-tuple-element.62) | copy-start | bytes 1572868
  222.6 2.3 copy-start.1
  224.8 2.3 %copy-start = (f32[8,64,1024]{2,1,0:T(8,128)S(1)}, f32[8,64,1024]{2,1,0:T(8,128)}, u32[]{:S(2)}) copy-start(f32[8,64,1024]{2,1,0:T(8,128)} %get-tuple-element.64) | copy-start | bytes 6291460

commit v2 on v0

v2 whole, which is shorter than its diff:
```python
import jax
import jax.numpy as jnp
from jax import lax
from jax.experimental import pallas as pl
from jax.experimental.pallas import tpu as pltpu
from jax.sharding import PartitionSpec as P

NORM_EPS = 1e-06
NEG_FILL = -1e30
F32 = jnp.float32
BF16 = jnp.bfloat16
MESH = pl.DeviceIdType.MESH
NT = (((1,), (1,)), ((), ()))
TN = (((0,), (0,)), ((), ()))
NN = (((1,), (0,)), ((), ()))
VMEM_LIMIT = 63 * 1024 * 1024


def dot(left, right, dims=NN):
    return lax.dot_general(left, right, dims, preferred_element_type=F32)


def lanes(start, size=128):
    return pl.ds(pl.multiple_of(start, 128), size)


class Place:
    def __init__(self):
        self.f = lax.axis_index("fsdp")
        self.s = lax.axis_index("seq")
        self.y = self.s // 4
        self.xl = (self.s // 2) % 2
        self.c = self.s % 2
        self.yp = (self.y + 1) % 4
        self.ym = (self.y + 3) % 4
        self.yo = (self.y + 2) % 4
        self.chip = self.s // 2
        self.j = self.y * 2 + self.c
        self.core = (self.f, self.slot(self.y, self.xl, 1 - self.c))
        self.xpart = (self.f, self.slot(self.y, 1 - self.xl, self.c))
        self.up = (self.f, self.slot(self.yp, self.xl, self.c))
        self.down = (self.f, self.slot(self.ym, self.xl, self.c))

    def slot(self, y, xl, c):
        return (y * 2 + xl) * 2 + c


def greet(me):
    barrier = pltpu.get_barrier_semaphore()
    for step in range(1, 8):
        pl.semaphore_signal(
            barrier, inc=1, device_id=((me.f + step) % 8, me.s), device_id_type=MESH
        )
    for step in range(1, 16):
        pl.semaphore_signal(
            barrier, inc=1, device_id=(me.f, (me.s + step) % 16), device_id_type=MESH
        )


def all_met():
    pl.semaphore_wait(pltpu.get_barrier_semaphore(), 22)


class Wire:
    def __init__(self, send_sem, recv_sem):
        self.send_sem, self.recv_sem = send_sem, recv_sem
        self.used = 0
        self.sent = []

    def send(self, src, dst, device):
        k = self.used
        self.used += 1
        copy = pltpu.make_async_remote_copy(
            src_ref=src,
            dst_ref=dst,
            send_sem=self.send_sem.at[k],
            recv_sem=self.recv_sem.at[k],
            device_id=device,
            device_id_type=MESH,
        )
        copy.start()
        self.sent.append(copy)
        return copy

    def drain(self):
        for copy in self.sent:
            copy.wait_send()
        self.sent = []


class Scatter:
    def __init__(self, me, send_sem, recv_sem, out, into):
        self.me, self.out, self.into = me, out, into
        self.send_sem, self.recv_sem = send_sem, recv_sem

    def copy(self, k, e, peer, arriving):
        return pltpu.make_async_remote_copy(
            src_ref=self.out.at[peer],
            dst_ref=self.into.at[peer if arriving else self.me.s],
            send_sem=self.send_sem.at[2 * k + e],
            recv_sem=self.recv_sem.at[2 * k + (e if arriving else self.me.c)],
            device_id=(self.me.f, peer),
            device_id_type=MESH,
        )

    def send(self, k):
        chip = (self.me.chip + 1 + k) % 8
        self.copy(k, 0, chip * 2, False).start()
        self.copy(k, 1, chip * 2 + 1, False).start()

    def keep(self, wire):
        me = self.me
        self.into[me.s] = self.out[me.s]
        other = me.s + 1 - 2 * me.c
        self.partner = wire.send(self.out.at[other], self.into.at[me.s], me.core)

    def finish(self):
        def collect(k, carry):
            there, back = (self.me.chip + 1 + k) % 8, (self.me.chip + 7 - k) % 8
            for e in range(2):
                self.copy(k, e, there * 2 + e, False).wait_send()
                self.copy(k, e, back * 2 + e, True).wait_recv()
            return carry

        lax.fori_loop(0, 7, collect, 0)
        self.partner.wait_recv()


def to_fsdp(wire, me, src_of, dst_of):
    copies = []
    for step in range(1, 8):
        peer = (me.f + step) % 8
        copies.append(wire.send(src_of(peer), dst_of(me.f), (peer, me.s)))
    return copies


def arrived(copies):
    for copy in copies:
        copy.wait_recv()


class Gather8:
    def __init__(self, wire, me, ref):
        self.wire, self.me, self.ref = wire, me, ref
        h = ref.shape[1] // 2
        self.head, self.tail = pl.ds(0, h), pl.ds(h, h)

    def slot(self, y):
        return y * 2 + self.me.c

    def push(self, y, part, device):
        at = self.ref.at[self.slot(y)] if part is None else self.ref.at[self.slot(y), part]
        return self.wire.send(at, at, device)

    def start(self):
        me = self.me
        self.up = [self.push(me.y, self.head, me.up)]
        self.down = [self.push(me.y, self.tail, me.down)]
        self.up.append(self.push(me.y, self.tail, me.up))
        self.down.append(self.push(me.y, self.head, me.down))
        self.cores = [self.push(me.y, None, me.core)]

    def relay(self):
        me = self.me
        self.up[0].wait_recv()
        self.far = [self.push(me.ym, self.head, me.up)]
        self.down[0].wait_recv()
        self.far.append(self.push(me.yp, self.tail, me.down))

    def middle(self):
        me = self.me
        self.up[1].wait_recv()
        self.cores.append(self.push(me.ym, None, me.core))
        self.down[1].wait_recv()
        self.cores.append(self.push(me.yp, None, me.core))

    def last(self):
        arrived(self.far)
        self.cores.append(self.push(self.me.yo, None, self.me.core))

    def finish(self):
        arrived(self.cores)


class Gather16:
    def __init__(self, wire, me, ref):
        self.wire, self.me, self.ref = wire, me, ref
        h = ref.shape[1] // 2
        self.head, self.tail = pl.ds(0, h), pl.ds(h, h)
        self.cores = []

    def slot(self, y, other):
        me = self.me
        return me.slot(y, 1 - me.xl if other else me.xl, me.c)

    def push(self, y, other, part, device):
        at = self.slot(y, other)
        at = self.ref.at[at] if part is None else self.ref.at[at, part]
        return self.wire.send(at, at, device)

    def to_core(self, y, other):
        self.cores.append((self.push(y, other, None, self.me.core), y, other))

    def spread(self, other):
        me = self.me
        up = [self.push(me.y, other, self.head, me.up)]
        down = [self.push(me.y, other, self.tail, me.down)]
        up.append(self.push(me.y, other, self.tail, me.up))
        down.append(self.push(me.y, other, self.head, me.down))
        return up, down

    def start(self):
        me = self.me
        self.cross = [self.push(me.y, False, part, me.xpart) for part in (self.head, self.tail)]
        self.near = [self.spread(False)]
        self.to_core(me.y, False)

    def relay(self, other):
        me = self.me
        up, down = self.near[int(other)]
        up[0].wait_recv()
        far = [self.push(me.ym, other, self.head, me.up)]
        down[0].wait_recv()
        far.append(self.push(me.yp, other, self.tail, me.down))
        return far

    def middle(self, other):
        up, down = self.near[int(other)]
        up[1].wait_recv()
        self.to_core(self.me.ym, other)
        down[1].wait_recv()
        self.to_core(self.me.yp, other)

    def run(self, use=lambda slot: None):
        me = self.me
        far_own = self.relay(False)
        arrived(self.cross)
        self.near.append(self.spread(True))
        self.to_core(me.y, True)
        use(self.slot(me.y, False))
        use(self.slot(me.y, True))
        self.middle(False)
        far_part = self.relay(True)
        use(self.slot(me.ym, False))
        use(self.slot(me.yp, False))
        arrived(far_own)
        self.to_core(me.yo, False)
        use(self.slot(me.yo, False))
        self.middle(True)
        use(self.slot(me.ym, True))
        use(self.slot(me.yp, True))
        for copy, y, other in self.cores[:4]:
            copy.wait_recv()
            use(me.slot(y, 1 - me.xl if other else me.xl, 1 - me.c))
        arrived(far_part)
        self.to_core(me.yo, True)
        use(self.slot(me.yo, True))
        for copy, y, other in self.cores[4:]:
            copy.wait_recv()
            use(me.slot(y, 1 - me.xl if other else me.xl, 1 - me.c))


class Reduce8:
    def __init__(self, wire, me, part, from_core, from_far, from_near):
        self.wire, self.me, self.part = wire, me, part
        self.from_core, self.from_far, self.from_near = from_core, from_far, from_near
        self.order = (me.yo, me.yp, me.ym, me.y)

    def start(self):
        me = self.me
        self.cores = []
        for d, y in enumerate(self.order):
            src = self.part.at[y * 2 + 1 - me.c]
            self.cores.append(self.wire.send(src, self.from_core.at[d], me.core))

    def combine(self, d):
        self.cores[d].wait_recv()
        own = self.part[self.order[d] * 2 + self.me.c]
        total = own.astype(F32) + self.from_core[d].astype(F32)
        self.from_core[d] = total.astype(BF16)

    def far(self):
        w, me, acc = self.wire, self.me, self.from_core
        h = acc.shape[1] // 2
        self.head, self.tail = pl.ds(0, h), pl.ds(h, h)
        self.combine(0)
        self.f_up = w.send(acc.at[0, self.head], self.from_far.at[0], me.up)
        self.f_down = w.send(acc.at[0, self.tail], self.from_far.at[1], me.down)
        self.combine(1)
        self.n_up = [w.send(acc.at[1, self.tail], self.from_near.at[0, self.tail], me.up)]
        self.combine(2)
        self.n_down = [w.send(acc.at[2, self.head], self.from_near.at[1, self.head], me.down)]

    def near(self):
        w, me, acc = self.wire, self.me, self.from_core
        self.f_up.wait_recv()
        total = acc[1, self.head].astype(F32) + self.from_far[0].astype(F32)
        acc[1, self.head] = total.astype(BF16)
        self.n_up.append(w.send(acc.at[1, self.head], self.from_near.at[0, self.head], me.up))
        self.f_down.wait_recv()
        total = acc[2, self.tail].astype(F32) + self.from_far[1].astype(F32)
        acc[2, self.tail] = total.astype(BF16)
        self.n_down.append(w.send(acc.at[2, self.tail], self.from_near.at[1, self.tail], me.down))

    def result(self):
        self.cores[3].wait_recv()
        own = self.part[self.me.y * 2 + self.me.c]
        total = own.astype(F32) + self.from_core[3].astype(F32)
        arrived(self.n_up)
        arrived(self.n_down)
        return total + self.from_near[0].astype(F32) + self.from_near[1].astype(F32)


def full_row(pv_all, row):
    return jnp.concatenate(
        [pv_all[f].astype(F32)[row : row + 1, :] for f in range(8)], axis=1
    )


def columns(pv_all, f):
    tile = jnp.concatenate([pv_all[f].astype(F32), jnp.zeros((112, 128), F32)], axis=0)
    return tile.T


def norm_stats(values):
    mean_val = jnp.mean(values, axis=-1, keepdims=True)
    centered = values - mean_val
    variance = jnp.mean(centered * centered, axis=-1, keepdims=True)
    inverse = lax.rsqrt(variance + NORM_EPS)
    return centered * inverse, inverse


def norm_back(cotangent, gain, normed, inverse):
    scaled = cotangent * gain
    first = jnp.mean(scaled, axis=-1, keepdims=True)
    second = jnp.mean(scaled * normed, axis=-1, keepdims=True)
    return inverse * (scaled - first - normed * second)


def column_sum(values):
    return jnp.sum(values, axis=0, keepdims=True)


def half_of(which, pair):
    return jnp.where(which == 0, pair[:, :64], pair[:, 64:])


def beside(which, half):
    zero = jnp.zeros_like(half)
    return jnp.where(
        which == 0,
        jnp.concatenate([half, zero], axis=1),
        jnp.concatenate([zero, half], axis=1),
    )


def fold(piece):
    return jnp.concatenate([piece[:64], piece[64:]], axis=1)


def unfold(packed):
    return jnp.concatenate([packed[:, :64], packed[:, 64:]], axis=0)


def three_parts(values):
    first = values.astype(BF16)
    rest = values - first.astype(F32)
    second = rest.astype(BF16)
    third = (rest - second.astype(F32)).astype(BF16)
    return first.astype(F32), second.astype(F32), third.astype(F32)


def eight(ref):
    total = ref[0].astype(F32)
    for f in range(1, 8):
        total = total + ref[f].astype(F32)
    return total


def layer(
    tok, gout, valid, w_qkv, w_proj, w_fc1, w_fc2, gain_in, shift_in, scale_in, bias_in,
    res, gtok, o_qkv, o_proj, o_fc1, w2_all, o_vec,
    nrm, grd, pv_all, v_all, wq_one, wq_all, wq_use, wp_all, w1_one, w1_all, wqf,
    qa, ka, va, ow, om, at,
    nmg, act, gpre, gn, mp, r_core, r_far, r_near, msg, gat, mid, gmid, atg, gac, gh,
    dw1, dw2, vec, db1,
    ga, qb, kt, dk, dv, dq, qm, qin, kvm, kvin, m_core, m_far, m_near,
    dwp, r1, r2, rp, x1, x2, xp, gp, dwq, rq, gq, vs, vr, vq,
    ss, rs, as_, ar_, bs, br,
):
    me = Place()
    wire = Wire(ss, rs)
    greet(me)
    vin = jnp.broadcast_to(valid[...].astype(F32), (16, 128)).astype(BF16)
    v_all[me.s] = vin
    bias = half_of(me.c, bias_in[:, lanes(me.y * 128)].astype(F32))
    pv_all[me.f] = jnp.concatenate(
        [
            gain_in[...].astype(F32),
            shift_in[...].astype(F32),
            scale_in[...].astype(F32),
            jnp.concatenate([bias, jnp.zeros((1, 64), F32)], axis=1),
            jnp.zeros((5, 128), F32),
        ],
        axis=0,
    ).astype(BF16)
    normed, _ = norm_stats(tok[...].astype(F32))
    nrm[me.s] = normed.astype(BF16)
    parts = [half_of(me.c, w_qkv[:, lanes(p * 1024 + me.chip * 128)]) for p in range(3)]
    wq_one[...] = jnp.concatenate([*parts, jnp.zeros((128, 64), BF16)], axis=1)
    wq_all[me.f] = wq_one[...]
    for f in range(0, 8, 2):
        pair = [half_of(me.c, w_fc1[:, lanes(g * 512 + me.y * 128)]) for g in (f, f + 1)]
        w1_one[:, f * 64 : (f + 2) * 64] = jnp.concatenate(pair, axis=1)
    w1_all[me.f] = w1_one[...]
    wp_all[me.f] = w_proj[...]
    wqf[me.f] = w_qkv[...]
    mine = pl.ds(pl.multiple_of(me.j * 64, 64), 64)
    w2_all[me.f] = w_fc2[mine]
    all_met()

    gather = Gather16(wire, me, nrm)
    gather.start()
    own_pv = pv_all.at[me.f]
    got_pv = to_fsdp(wire, me, lambda p: own_pv, lambda f: pv_all.at[f])
    got_wq = to_fsdp(wire, me, lambda p: wq_one, lambda f: wq_all.at[f])
    got_v = []
    for step in range(1, 16):
        peer = (me.s + step) % 16
        got_v.append(wire.send(v_all.at[me.s], v_all.at[me.s], (me.f, peer)))
    half = pl.ds(pl.multiple_of(me.c * 64, 64), 64)

    far_own = None
    ready = {}

    def prepare():
        arrived(got_pv)
        arrived(got_wq)
        shifts = jnp.zeros((1, 256), F32)
        for f in range(8):
            cols = columns(pv_all, f)
            weight = wq_all[f]
            wq_use[f * 128 : (f + 1) * 128, :] = (weight.astype(F32) * cols[:, 0:1]).astype(BF16)
            row = jnp.broadcast_to(pv_all[f].astype(F32)[2:3, :], (16, 128)).astype(BF16)
            shifts = shifts + dot(row, weight)[0:1]
        own = half_of(me.c, pv_all[me.chip].astype(F32))
        zero = jnp.zeros((1, 64), F32)
        ready["bias"] = shifts + jnp.concatenate([own[4:5], zero, own[5:6], zero], axis=1)
        ready["wp"] = to_fsdp(
            wire, me, lambda p: w_proj.at[half], lambda f: wp_all.at[f, half]
        )
        ready["w1"] = to_fsdp(wire, me, lambda p: w1_one, lambda f: w1_all.at[f])
        arrived(got_v)
        flags = v_all[:, 0, :].astype(F32)
        flags = jnp.concatenate([flags, jnp.zeros((112, 128), F32)], axis=0).T
        lane = lax.broadcasted_iota(jnp.int32, (128, 64), 1)
        for blk in range(16):
            mask = (1.0 - flags[:, blk : blk + 1]) * NEG_FILL
            ext = jnp.where(lane == 0, mask, jnp.where(lane < 4, 1.0, 0.0))
            ka[blk * 128 : (blk + 1) * 128, 64:] = ext.astype(BF16)

    ext_lane = lax.broadcasted_iota(jnp.int32, (128, 64), 1)
    q_ext = jnp.where(ext_lane == 0, 1.0, 0.0).astype(BF16)
    v_ext = jnp.where(ext_lane < 3, 1.0, 0.0).astype(BF16)

    def project(slot):
        if not ready:
            prepare()
        qkv = dot(nrm[slot], wq_use[...]) + ready["bias"]
        rows = pl.ds(pl.multiple_of(slot * 128, 128), 128)
        query = (qkv[:, :64].astype(BF16) * 0.125).astype(BF16)
        qa[rows, :] = jnp.concatenate([query, q_ext], axis=1)
        ka[rows, :64] = qkv[:, 64:128].astype(BF16)
        va[rows, :] = jnp.concatenate([qkv[:, 128:192].astype(BF16), v_ext], axis=1)

    gather.run(project)
    grd[me.j] = (full_row(pv_all, 9) * gout[...].astype(F32)).astype(BF16)
    grad_gather = Gather8(wire, me, grd)
    grad_gather.start()
    got_w2 = to_fsdp(wire, me, lambda p: w_fc2.at[mine], lambda f: w2_all.at[f])

    heads_out = Scatter(me, as_, ar_, om, at)
    out_lane = lax.broadcasted_iota(jnp.int32, (256, 128), 1)

    def attend(k):
        chip = (me.chip + 1 + k) % 8
        rows = pl.ds(pl.multiple_of(chip * 256, 256), 256)
        scores = dot(qa[rows, :], ka[...], NT)
        row_max = jnp.max(scores, axis=1, keepdims=True)
        terms = jnp.exp(scores - row_max).astype(BF16)
        mixed = dot(terms, va[...])
        total = mixed[:, 64:65]
        heads = mixed / total
        log_sum = row_max + jnp.log(total)
        ow[rows, :] = jnp.where(out_lane < 64, heads, log_sum)
        rounded = heads[:, :64].astype(BF16)
        for e in range(2):
            om[chip * 2 + e] = fold(rounded[e * 128 : (e + 1) * 128])

    def attend_send(k, carry):
        attend(k)
        heads_out.send(k)
        return carry

    lax.fori_loop(0, 2, attend_send, 0)
    grad_gather.relay()
    lax.fori_loop(2, 5, attend_send, 0)
    grad_gather.middle()
    lax.fori_loop(5, 7, attend_send, 0)
    grad_gather.last()
    arrived(ready["wp"])
    swap = [wire.send(wp_all.at[f, half], wp_all.at[f, half], me.core) for f in range(8)]
    attend(7)
    heads_out.keep(wire)
    heads_out.finish()

    attn_tok = jnp.concatenate([unfold(at[h]) for h in range(16)], axis=1)
    atg[me.j] = attn_tok
    arrived(swap)
    scale_one = full_row(pv_all, 8)
    branch = dot(attn_tok, wp_all[...].reshape(1024, 1024)) + full_row(pv_all, 6)
    middle = tok[...].astype(F32) + scale_one * branch
    mid[...] = middle
    normed, inverse = norm_stats(middle)
    gain = full_row(pv_all, 1)
    nmg[me.j] = (normed * gain + full_row(pv_all, 3)).astype(BF16)
    gather = Gather8(wire, me, nmg)
    gather.start()
    attn_gather = Gather8(wire, me, atg)
    grad_gather.finish()
    gather.relay()
    gather.middle()
    attn_gather.start()
    gather.last()
    arrived(ready["w1"])
    arrived(got_w2)
    got_wqf = to_fsdp(wire, me, lambda p: w_qkv.at[half], lambda f: wqf.at[f, half])
    bias_one = jnp.concatenate(
        [pv_all[f].astype(F32)[10:11, :64] for f in range(8)], axis=1
    )
    gather.finish()

    def feed(b, carry):
        two = pl.ds(2 * b, 2)
        rows = pl.ds(pl.multiple_of(b * 256, 256), 256)
        w1 = w1_all[...].reshape(1024, 512)
        w2 = w2_all[...].reshape(512, 1024)
        pre = dot(nmg[two].reshape(256, 1024), w1) + bias_one
        cdf = 0.5 * (1.0 + lax.erf(pre * 0.7071067811865476))
        acts = (pre * cdf).astype(BF16)
        act[rows, :] = acts
        mp[two] = dot(acts, w2).astype(BF16).reshape(2, 128, 1024)
        grad_act = dot(grd[two].reshape(256, 1024), w2, NT)
        slope = cdf + pre * jnp.exp(-0.5 * pre * pre) * 0.3989422804014327
        grad_pre = (grad_act * slope).astype(BF16)
        gpre[rows, :] = grad_pre
        gn[two] = dot(grad_pre, w1, NT).astype(BF16).reshape(2, 128, 1024)
        return carry + column_sum(grad_pre.astype(F32))

    db1[...] = lax.fori_loop(0, 4, feed, jnp.zeros((1, 512), F32))
    reduce = Reduce8(wire, me, gn, r_core, r_far, r_near)
    reduce.start()
    reduce.far()
    attn_gather.relay()
    dw2[...] = dot(act[...], grd[...].reshape(1024, 1024), TN).astype(BF16).reshape(8, 64, 1024)
    reduce.near()
    got = to_fsdp(wire, me, lambda p: dw2.at[p], lambda f: r2.at[f])
    dw1[...] = dot(nmg[...].reshape(1024, 1024), gpre[...], TN).astype(BF16).reshape(8, 128, 512)
    got += to_fsdp(wire, me, lambda p: dw1.at[p], lambda f: r1.at[f])
    r1[me.f] = dw1[me.f]
    r2[me.f] = dw2[me.f]
    cotangent = reduce.result()
    grad_middle = gout[...].astype(F32) + norm_back(cotangent, gain, normed, inverse)
    gmid[...] = grad_middle
    grad_attn = (scale_one * grad_middle).astype(BF16)
    gat[...] = grad_attn
    grad_tok = dot(grad_attn, wp_all[...].reshape(1024, 1024), NT).astype(BF16)
    for h in range(16):
        msg[h] = fold(grad_tok[:, h * 64 : (h + 1) * 64])
    gh[me.s] = msg[me.s]
    got_gh = []
    for step in range(1, 16):
        peer = (me.s + step) % 16
        got_gh.append(wire.send(msg.at[peer], gh.at[me.s], (me.f, peer)))
    got_gac = []
    for step in range(1, 8):
        peer = (me.j + step) % 8
        device = (me.f, me.slot(peer // 2, me.xl, peer % 2))
        got_gac.append(wire.send(gat.at[:, lanes(peer * 128)], gac.at[me.j], device))
    gac[me.j] = gat[:, lanes(me.j * 128)]
    mlp = Reduce8(wire, me, mp, m_core, m_far, m_near)
    mlp.start()
    zero = jnp.zeros((1, 1024), F32)
    vec[...] = jnp.concatenate(
        [
            zero,
            column_sum(cotangent * normed),
            zero,
            column_sum(cotangent),
            zero,
            zero,
            column_sum(grad_attn.astype(F32)),
            column_sum(grd[me.j].astype(F32)),
            column_sum(grad_middle * branch),
            jnp.zeros((7, 1024), F32),
        ],
        axis=0,
    )
    attn_gather.middle()
    attn_gather.last()
    mlp.far()
    lane = lax.broadcasted_iota(jnp.int32, (128, 128), 1)
    for blk in range(16):
        rows = slice(blk * 128, (blk + 1) * 128)
        l1, l2, l3 = three_parts(-ow[rows, 64:65])
        wide = qa[rows, :].astype(F32)
        wide = jnp.where(lane == 65, l1, wide)
        wide = jnp.where(lane == 66, l2, wide)
        wide = jnp.where(lane == 67, l3, wide)
        qb[rows, :] = wide.astype(BF16)
        kt[:, rows] = ka[rows, :].astype(F32).T.astype(BF16)
    dk[...] = jnp.zeros_like(dk)
    dv[...] = jnp.zeros_like(dv)

    arrived(got_gh)
    for blk in range(16):
        rows = slice(blk * 128, (blk + 1) * 128)
        grad = unfold(gh[blk])
        delta = jnp.sum(grad.astype(F32) * ow[rows, :64], axis=1, keepdims=True)
        d1, d2, d3 = three_parts(-delta)
        wide = jnp.concatenate([grad, jnp.zeros((128, 64), BF16)], axis=1).astype(F32)
        wide = jnp.where(lane == 64, d1, wide)
        wide = jnp.where(lane == 65, d2, wide)
        wide = jnp.where(lane == 66, d3, wide)
        ga[rows, :] = wide.astype(BF16)

    queries_out = Scatter(me, bs, br, qm, qin)

    def back(k):
        chip = (me.chip + 1 + k) % 8
        rows = pl.ds(pl.multiple_of(chip * 256, 256), 256)
        query, grad = qb[rows, :], ga[rows, :]
        probs = jnp.exp(dot(ka[...], query, NT))
        dv[...] += dot(probs.astype(BF16), grad)
        slope = dot(va[...], grad, NT)
        scores = (probs * slope).astype(BF16)
        dk[...] += dot(scores, query)
        turned = dot(kt[...], scores)
        grad_query = (turned.T[:, :64] * 0.125).astype(BF16)
        dq[rows, :64] = grad_query
        for e in range(2):
            qm[chip * 2 + e] = fold(grad_query[e * 128 : (e + 1) * 128])

    def back_send(k, carry):
        back(k)
        queries_out.send(k)
        return carry

    lax.fori_loop(0, 3, back_send, 0)
    mlp.near()
    arrived(got_gac)
    attn_gather.finish()
    for f in range(8):
        tok_cols = atg[:, :, f * 128 : (f + 1) * 128].reshape(1024, 128)
        dwp[f] = dot(tok_cols, gac[...].reshape(1024, 128), TN).astype(BF16)
    got += to_fsdp(wire, me, lambda p: dwp.at[p], lambda f: rp.at[f])
    rp[me.f] = dwp[me.f]
    arrived(got_wqf)
    swap = [wire.send(wqf.at[f, half], wqf.at[f, half], me.core) for f in range(8)]
    lax.fori_loop(3, 6, back_send, 0)
    arrived(got)
    x1[0] = eight(r1).astype(BF16)
    x2[0] = eight(r2).astype(BF16)
    xp[0] = eight(rp).astype(BF16)
    crossed = [wire.send(x.at[0], x.at[1], me.xpart) for x in (x1, x2, xp)]
    lax.fori_loop(6, 7, back_send, 0)
    back(7)
    queries_out.keep(wire)

    for blk in range(16):
        rows = slice(blk * 128, (blk + 1) * 128)
        grad_key, grad_value = dk[rows, :64].astype(BF16), dv[rows, :64].astype(BF16)
        kvm[blk] = jnp.concatenate([grad_key, grad_value], axis=1)
        dq[rows, 64:128] = grad_key
        dq[rows, 128:] = jnp.concatenate([grad_value, jnp.zeros((128, 64), BF16)], axis=1)
    got_kv = []
    for step in range(1, 16):
        peer = (me.s + step) % 16
        got_kv.append(wire.send(kvm.at[peer], kvin.at[me.s], (me.f, peer)))
    kvin[me.s] = kvm[me.s]

    mlp_out = mlp.result() + full_row(pv_all, 7)
    res[...] = (mid[...] + full_row(pv_all, 9) * mlp_out).astype(BF16)
    vec[9:10, :] = column_sum(gout[...].astype(F32) * mlp_out)
    sums = column_sum(dq[...].astype(F32))
    got_q, got_vec = [], []
    for step in range(1, 9):
        f = (me.f + step) % 8
        cols = columns(pv_all, f)
        product = dot(nrm[:, :, lanes(f * 128)].reshape(2048, 128), dq[...], TN)
        grad_wq = product * cols[:, 0:1] + cols[:, 2:3] * sums
        weight = wq_all[f].astype(F32)
        first = jnp.sum(weight * product, axis=1, keepdims=True)
        second = jnp.sum(weight * sums, axis=1, keepdims=True)
        turned = jnp.where(lane == 0, first, jnp.where(lane == 1, second, 0.0)).T
        rows = vec[:, lanes(f * 128)]
        piece = half_of(f % 2, db1[:, lanes((f // 2) * 128)])
        bias = beside(me.c, piece)
        here = me.chip == f
        packed = jnp.concatenate(
            [
                turned[0:1],
                rows[1:2],
                turned[1:2],
                rows[3:4],
                jnp.where(here, beside(me.c, sums[:, :64]), 0.0),
                jnp.where(here, beside(me.c, sums[:, 128:192]), 0.0),
                rows[6:10],
                *[jnp.where(me.y == y, bias, 0.0) for y in range(4)],
                jnp.zeros((2, 128), F32),
            ],
            axis=0,
        )
        if step < 8:
            dwq[f] = grad_wq.astype(BF16)
            vs[f] = packed
            got_q.append(wire.send(dwq.at[f], rq.at[me.f], (f, me.s)))
            got_vec.append(wire.send(vs.at[f], vr.at[me.f], (f, me.s)))
        else:
            rq[me.f] = grad_wq.astype(BF16)
            vr[me.f] = packed

    arrived(crossed)
    gathers = []
    for x, g in ((x1, w1_all), (x2, w2_all), (xp, gp)):
        g[me.j] = (x[0].astype(F32) + x[1].astype(F32)).astype(BF16)
        gathers.append(Gather8(wire, me, g))
    for gather in gathers:
        gather.start()

    queries_out.finish()
    arrived(got_kv)
    arrived(swap)
    parts = [unfold(qin[h]) for h in range(16)]
    parts += [kvin[h][:, :64] for h in range(16)] + [kvin[h][:, 64:] for h in range(16)]
    grad_qkv = jnp.concatenate(parts, axis=1)
    cotangent = dot(grad_qkv, wqf[...].reshape(1024, 3072), NT)

    arrived(got_q)
    gq[me.s] = eight(rq).astype(BF16)
    gather_q = Gather16(wire, me, gq)
    gather_q.start()
    arrived(got_vec)
    vq[me.s] = eight(vr)
    got_vq = []
    for step in range(1, 16):
        peer = (me.s + step) % 16
        got_vq.append(wire.send(vq.at[me.s], vq.at[me.s], (me.f, peer)))
    for gather in gathers:
        gather.relay()
    for gather in gathers:
        gather.middle()
    normed, inverse = norm_stats(tok[...].astype(F32))
    gtok[...] = gmid[...] + norm_back(cotangent, full_row(pv_all, 0), normed, inverse)
    for gather in gathers:
        gather.last()
    gather_q.run()
    for part in range(3):
        cols = slice(part * 64, (part + 1) * 64)
        for k in range(8):
            pair = jnp.concatenate([gq[2 * k, :, cols], gq[2 * k + 1, :, cols]], axis=1)
            o_qkv[:, part * 1024 + k * 128 : part * 1024 + (k + 1) * 128] = pair
    for gather in gathers:
        gather.finish()
    for j in range(8):
        o_proj[:, j * 128 : (j + 1) * 128] = gp[j]
    for f in range(8):
        cols = slice(f * 64, (f + 1) * 64)
        for k in range(4):
            pair = jnp.concatenate([w1_all[2 * k, :, cols], w1_all[2 * k + 1, :, cols]], axis=1)
            o_fc1[:, f * 512 + k * 128 : f * 512 + (k + 1) * 128] = pair
    arrived(got_vq)
    total = vq[0]
    for s in range(1, 16):
        total = total + vq[s]
    o_vec[...] = total
    wire.drain()


OUTS = (
    ((128, 1024), BF16),
    ((128, 1024), F32),
    ((128, 3072), BF16),
    ((128, 1024), BF16),
    ((128, 4096), BF16),
    ((8, 64, 1024), BF16),
    ((16, 128), F32),
)
SCRATCH = (
    ((16, 128, 1024), BF16),
    ((8, 128, 1024), BF16),
    ((8, 16, 128), BF16),
    ((16, 16, 128), BF16),
    ((128, 256), BF16),
    ((8, 128, 256), BF16),
    ((1024, 256), BF16),
    ((8, 128, 1024), BF16),
    ((128, 512), BF16),
    ((8, 128, 512), BF16),
    ((8, 128, 3072), BF16),
    ((2048, 128), BF16),
    ((2048, 128), BF16),
    ((2048, 128), BF16),
    ((2048, 128), F32),
    ((16, 64, 128), BF16),
    ((16, 64, 128), BF16),
    ((8, 128, 1024), BF16),
    ((1024, 512), BF16),
    ((1024, 512), BF16),
    ((8, 128, 1024), BF16),
    ((8, 128, 1024), BF16),
    ((4, 128, 1024), BF16),
    ((2, 64, 1024), BF16),
    ((2, 128, 1024), BF16),
    ((16, 64, 128), BF16),
    ((128, 1024), BF16),
    ((128, 1024), F32),
    ((128, 1024), F32),
    ((8, 128, 1024), BF16),
    ((8, 128, 128), BF16),
    ((16, 64, 128), BF16),
    ((8, 128, 512), BF16),
    ((8, 64, 1024), BF16),
    ((16, 1024), F32),
    ((1, 512), F32),
    ((2048, 128), BF16),
    ((2048, 128), BF16),
    ((128, 2048), BF16),
    ((2048, 128), F32),
    ((2048, 128), F32),
    ((2048, 256), BF16),
    ((16, 64, 128), BF16),
    ((16, 64, 128), BF16),
    ((16, 128, 128), BF16),
    ((16, 128, 128), BF16),
    ((4, 128, 1024), BF16),
    ((2, 64, 1024), BF16),
    ((2, 128, 1024), BF16),
    ((8, 128, 128), BF16),
    ((8, 128, 512), BF16),
    ((8, 64, 1024), BF16),
    ((8, 128, 128), BF16),
    ((2, 128, 512), BF16),
    ((2, 64, 1024), BF16),
    ((2, 128, 128), BF16),
    ((8, 128, 128), BF16),
    ((8, 128, 256), BF16),
    ((8, 128, 256), BF16),
    ((16, 128, 256), BF16),
    ((8, 16, 128), F32),
    ((8, 16, 128), F32),
    ((16, 16, 128), F32),
)
COPIES = 352


def body(
    tokens, image_ids, valid, w_qkv, w_proj, w_fc1, w_fc2,
    norm_gain, shifts, layer_scale, fc1_bias, grad_out,
):
    semaphores = [pltpu.SemaphoreType.DMA((n,)) for n in (COPIES, COPIES, 14, 14, 14, 14)]
    whole = pl.BlockSpec(memory_space=pltpu.VMEM)
    res, gtok, g_qkv, g_proj, g_fc1, g_fc2, g_vec = pl.pallas_call(
        layer,
        out_shape=[jax.ShapeDtypeStruct(shape, dtype) for shape, dtype in OUTS],
        in_specs=[whole] * 11,
        out_specs=[whole] * len(OUTS),
        scratch_shapes=[pltpu.VMEM(shape, dtype) for shape, dtype in SCRATCH] + semaphores,
        name="layer",
        compiler_params=pltpu.CompilerParams(
            collective_id=1, has_side_effects=True, vmem_limit_bytes=VMEM_LIMIT
        ),
    )(
        tokens, grad_out, valid.reshape(1, 128), w_qkv[0], w_proj[0], w_fc1[0], w_fc2[0],
        norm_gain[0], shifts[0], layer_scale[0], fc1_bias,
    )
    return (
        res,
        gtok,
        g_qkv[None].astype(F32),
        g_proj[None].astype(F32),
        g_fc1[None].astype(F32),
        g_fc2.reshape(1, 512, 1024).astype(F32),
        g_vec[None, 0:2],
        g_vec[None, 2:8],
        g_vec[None, 8:10],
        g_vec[10:14].reshape(1, 512),
    )


def solution(mesh):
    rows = P(("fsdp", "seq"), None)
    flat = P(("fsdp", "seq"))
    mats = P(None, "fsdp", None)
    vecs = P(None, None, "fsdp")
    bias = P(None, "fsdp")
    return jax.shard_map(
        body,
        mesh=mesh,
        in_specs=(rows, flat, flat, mats, mats, mats, mats, vecs, vecs, vecs, bias, rows),
        out_specs=(rows, rows, mats, mats, mats, mats, vecs, vecs, vecs, bias),
        check_vma=False,
    )
```

time: 1070 us -> 209 us (0.20)
  waiting for transfers between devices: 658 us -> 0 us
  Pallas kernels: 0 us -> 196 us
  blocking collectives: 184 us -> 0 us
  matrix products: 115 us -> 0 us
  starting transfers between devices: 32.8 us -> 0 us
  local copies, waits for them, and re-layouts: 30.6 us -> 5.38 us
  between operations: 15.6 us -> 0.67 us
  loops' own time: 13.6 us -> 0 us
    reduce_scatter x4 -> x0, waiting for transfers between devices: 300 us -> none  [the longest x2 184 us: reduce_terms(): lax.psum_scatter(terms[0].astype(jnp.bfloat16), 'fsdp', scatter_dimension...]
    pallas_call x0 -> x1, Pallas kernels: none -> 196 us  [body(): pl.pallas_call(layer, out_shape=[jax.ShapeDtypeStruct(shape, dtype) for s...]
    all_gather x4 -> x0, waiting for transfers between devices: 170 us -> none  [the longest x1 103 us: fetch_layer(): lax.all_gather(pieces[3], 'fsdp', axis=0, tiled=True)]
    all_gather x6 -> x0, blocking collectives: 128 us -> none  [the longest x1 26.3 us: fetch_layer(): lax.all_gather(pieces[7], 'fsdp', axis=0, tiled=True)]
    dot_general x40 -> x0, matrix products: 115 us -> none  [the longest x8 22 us: block_scores(): jnp.einsum('qhd,khd->hqk', query_blk, key_h, preferred_element_type=jnp.f...]
    psum x1 -> x0, waiting for transfers between devices: 100 us -> none  [reduce_terms(): lax.psum(shares[0].astype(jnp.bfloat16), 'seq').astype(jnp.float32)]
    unnamed x11 -> x0, waiting for transfers between devices: 55.4 us -> none
    all_to_all x7 -> x0, starting transfers between devices: 32 us -> none  [the longest x1 5.39 us: backward_layer(): lax.all_to_all(grad_attn_tok, 'seq', split_axis=1, concat_axis=0, tiled=T...]
  transfers between devices with their start and end apart: 17 -> 0, of which waited for: 13 -> 0; matrix products, arithmetic and copies ran while one was open for 12% -> 0% of each run, Pallas kernels for 0% -> 0%
where the time goes in v2:
time: 209 us
  Pallas kernels  196 us (94%)
  other arithmetic  6.45 us (3%)
  local copies, waits for them, and re-layouts  5.38 us (3%)
    pallas_call x1, Pallas kernels, body(): pl.pallas_call(layer, out_shape=[jax.ShapeDtypeStruct(shape, dtype) for s...  196 us

profile of v2, /device:TPU:1, one launch (start us, length us, event | category | flops | bytes accessed | tf_op | source)
XLA Modules:
  0.0 209.0 jit_solution(13580076847131042916)
XLA Ops:
  0.6 196.5 %layer.1 = (bf16[128,1024]{1,0:T(8,128)(2,1)}, f32[128,1024]{1,0:T(8,128)}, bf16[128,3072]{1,0:T(8,128)(2,1)}, bf16[128,1024]{1,0:T(8,128)(2,1)}, bf16[128,4096]...) custom-call(bf16[128,1024]{1,0:T(8,128)(2,1)} %tok.1, bf16[128,1024]{1,0:T(8,128)(2,1)} %gout.1, ...), custom_call_target="tpu_custom_call" | custom-call | tf_op jit(solution)/shard_map/layer/pallas_call | solution.py:873
  197.1 0.0 copy-start
  197.1 1.3 slice_bitcast_fusion.1
  198.5 0.7 slice_bitcast_fusion
  199.2 0.6 copy.21
  199.8 1.3 slice.15
  201.0 2.8 %bitcast_convert_fusion = f32[1,512,1024]{2,1,0:T(8,128)} fusion(bf16[1,512,1024]{2,1,0:T(8,128)(2,1)} %bitcast.30), kind=kLoop, calls=%fused_computation | loop fusion | flops 524288 | bytes 3145728 | tf_op jit(solution)/shard_map/convert_element_type | solution.py:893
  203.8 0.0 copy-start.1
  203.8 0.0 copy-done
  203.8 0.0 copy-start.3
  203.8 1.5 bitcast_convert_fusion.1
  205.3 0.0 copy-start.4
  205.3 0.0 copy-start.2
  205.3 0.0 copy-done.1
  205.3 1.3 bitcast_convert_fusion.2
  206.6 0.0 copy-done.3
  206.6 0.8 bitcast_convert_fusion.3
  207.5 0.0 copy-done.4
  207.5 0.7 copy.24
  208.2 0.0 copy-done.2
  208.2 0.8 copy.25
Async XLA Ops:
  197.1 6.7 %copy-start = (bf16[128,4096]{1,0:T(8,128)(2,1)S(1)}, bf16[128,4096]{1,0:T(8,128)(2,1)}, u32[]{:S(2)}) copy-start(bf16[128,4096]{1,0:T(8,128)(2,1)} %get-tuple-element.21) | copy-start | bytes 3145732
  203.8 1.5 copy-start.1
  203.8 2.8 %copy-start.3 = (bf16[128,1024]{1,0:T(8,128)(2,1)S(1)}, bf16[128,1024]{1,0:T(8,128)(2,1)}, u32[]{:S(2)}) copy-start(bf16[128,1024]{1,0:T(8,128)(2,1)} %get-tuple-element.20) | copy-start | bytes 786436
  205.3 2.2 %copy-start.4 = (bf16[128,1024]{1,0:T(8,128)(2,1)S(1)}, bf16[128,1024]{1,0:T(8,128)(2,1)}, u32[]{:S(2)}) copy-start(bf16[128,1024]{1,0:T(8,128)(2,1)} %get-tuple-element.46) | copy-start | bytes 786436
  205.3 2.9 %copy-start.2 = (f32[128,1024]{1,0:T(8,128)S(1)}, f32[128,1024]{1,0:T(8,128)}, u32[]{:S(2)}) copy-start(f32[128,1024]{1,0:T(8,128)} %get-tuple-element.47) | copy-start | bytes 1572868

commit v3 on v2

--- a/solution.py
+++ b/solution.py
@@ -82,10 +82,14 @@
         self.sent.append(copy)
         return copy
 
+    def settle(self, copies):
+        for copy in copies:
+            copy.wait_send()
+        done = {id(copy) for copy in copies}
+        self.sent = [copy for copy in self.sent if id(copy) not in done]
+
     def drain(self):
-        for copy in self.sent:
-            copy.wait_send()
-        self.sent = []
+        self.settle(list(self.sent))
 
 
 class Scatter:
@@ -139,6 +143,71 @@
         copy.wait_recv()
 
 
+class Fan:
+    def __init__(self, wire, me, src, dst):
+        self.wire, self.me, self.src, self.dst = wire, me, src, dst
+
+    def at(self, dz, other=False):
+        z, xh = self.me.f // 2, self.me.f % 2
+        return ((z + dz) % 4) * 2 + (1 - xh if other else xh)
+
+    def push(self, src, dst, f):
+        return self.wire.send(src, dst, (f, self.me.s))
+
+    def start(self):
+        slot = self.dst(self.me.f)
+        self.cross = self.push(self.src, slot, self.at(0, True))
+        self.near = [self.push(self.src, slot, self.at(dz)) for dz in (1, 3)]
+        self.far = self.push(self.src, slot, self.at(2))
+
+    def relay_near(self):
+        self.cross.wait_recv()
+        slot = self.dst(self.at(0, True))
+        self.near += [self.push(slot, slot, self.at(dz)) for dz in (1, 3)]
+
+    def relay_far(self):
+        self.far.wait_recv()
+        slot = self.dst(self.at(2))
+        self.near.append(self.push(slot, slot, self.at(0, True)))
+
+    def finish(self):
+        arrived(self.near)
+
+    def settle(self):
+        self.wire.settle([self.cross, self.far, *self.near])
+
+
+class FanIn(Fan):
+    def __init__(self, wire, me, part, into):
+        self.wire, self.me, self.part, self.into = wire, me, part, into
+
+    def start(self):
+        part, into = self.part, self.into
+        self.over = [self.push(part.at[self.at(2, True)], into.at[6], self.at(0, True))]
+        for k, dz in enumerate((1, 3)):
+            self.over.append(self.push(part.at[self.at(dz, True)], into.at[4 + k], self.at(dz)))
+        self.last = []
+        for k, dz in enumerate((1, 3)):
+            self.last.append(self.push(part.at[self.at(dz)], into.at[1 + k], self.at(dz)))
+
+    def forward(self):
+        part, into = self.part, self.into
+        arrived(self.over)
+        total = into[4].astype(F32) + into[5].astype(F32) + part[self.at(0, True)].astype(F32)
+        into[4] = total.astype(BF16)
+        self.last.append(self.push(into.at[4], into.at[0], self.at(0, True)))
+        total = into[6].astype(F32) + part[self.at(2)].astype(F32)
+        into[6] = total.astype(BF16)
+        self.last.append(self.push(into.at[6], into.at[3], self.at(2)))
+
+    def result(self):
+        arrived(self.last)
+        total = self.part[self.me.f].astype(F32)
+        for k in range(4):
+            total = total + self.into[k].astype(F32)
+        return total
+
+
 class Gather8:
     def __init__(self, wire, me, ref):
         self.wire, self.me, self.ref = wire, me, ref
@@ -231,31 +300,33 @@
         down[1].wait_recv()
         self.to_core(self.me.yp, other)
 
-    def run(self, use=lambda slot: None):
+    def run(self, crossed=lambda: None, prepare=lambda: None, use=lambda slot: None):
         me = self.me
         far_own = self.relay(False)
         arrived(self.cross)
         self.near.append(self.spread(True))
         self.to_core(me.y, True)
+        crossed()
+        self.middle(False)
+        far_part = self.relay(True)
+        arrived(far_own)
+        self.to_core(me.yo, False)
+        prepare()
         use(self.slot(me.y, False))
         use(self.slot(me.y, True))
-        self.middle(False)
-        far_part = self.relay(True)
         use(self.slot(me.ym, False))
         use(self.slot(me.yp, False))
-        arrived(far_own)
-        self.to_core(me.yo, False)
+        self.middle(True)
         use(self.slot(me.yo, False))
-        self.middle(True)
-        use(self.slot(me.ym, True))
-        use(self.slot(me.yp, True))
-        for copy, y, other in self.cores[:4]:
+        for copy, y, other in self.cores[:3]:
             copy.wait_recv()
             use(me.slot(y, 1 - me.xl if other else me.xl, 1 - me.c))
         arrived(far_part)
         self.to_core(me.yo, True)
+        use(self.slot(me.ym, True))
+        use(self.slot(me.yp, True))
         use(self.slot(me.yo, True))
-        for copy, y, other in self.cores[4:]:
+        for copy, y, other in self.cores[3:]:
             copy.wait_recv()
             use(me.slot(y, 1 - me.xl if other else me.xl, 1 - me.c))
 
@@ -379,20 +450,21 @@
 
 def layer(
     tok, gout, valid, w_qkv, w_proj, w_fc1, w_fc2, gain_in, shift_in, scale_in, bias_in,
-    res, gtok, o_qkv, o_proj, o_fc1, w2_all, o_vec,
-    nrm, grd, pv_all, v_all, wq_one, wq_all, wq_use, wp_all, w1_one, w1_all, wqf,
+    res, gtok, gq, gp, w1_all, w2_all, o_vec,
+    nrm, grd, pv_all, v_all, wq_one, wq_all, wq_use, wp_all, w1_one, wqf,
     qa, ka, va, ow, om, at,
     nmg, act, gpre, gn, mp, r_core, r_far, r_near, msg, gat, mid, gmid, atg, gac, gh,
     dw1, dw2, vec, db1,
-    ga, qb, kt, dk, dv, dq, qm, qin, kvm, kvin, m_core, m_far, m_near,
-    dwp, r1, r2, rp, x1, x2, xp, gp, dwq, rq, gq, vs, vr, vq,
-    ss, rs, as_, ar_, bs, br,
+    ga, qb, kt, dk, dv, dqt, wqt, qm, qin, kvm, kvin, m_core, m_far, m_near,
+    dwp, r1, r2, rp, x1, x2, xp, dwq, rq, vs, vr, vq,
+    ss, rs, as_, ar_, bs, br, own_sem,
 ):
     me = Place()
     wire = Wire(ss, rs)
     greet(me)
-    vin = jnp.broadcast_to(valid[...].astype(F32), (16, 128)).astype(BF16)
-    v_all[me.s] = vin
+    normed, _ = norm_stats(tok[...].astype(F32))
+    nrm[me.s] = normed.astype(BF16)
+    v_all[me.s] = jnp.broadcast_to(valid[...].astype(F32), (16, 128)).astype(BF16)
     bias = half_of(me.c, bias_in[:, lanes(me.y * 128)].astype(F32))
     pv_all[me.f] = jnp.concatenate(
         [
@@ -404,19 +476,8 @@
         ],
         axis=0,
     ).astype(BF16)
-    normed, _ = norm_stats(tok[...].astype(F32))
-    nrm[me.s] = normed.astype(BF16)
     parts = [half_of(me.c, w_qkv[:, lanes(p * 1024 + me.chip * 128)]) for p in range(3)]
     wq_one[...] = jnp.concatenate([*parts, jnp.zeros((128, 64), BF16)], axis=1)
-    wq_all[me.f] = wq_one[...]
-    for f in range(0, 8, 2):
-        pair = [half_of(me.c, w_fc1[:, lanes(g * 512 + me.y * 128)]) for g in (f, f + 1)]
-        w1_one[:, f * 64 : (f + 2) * 64] = jnp.concatenate(pair, axis=1)
-    w1_all[me.f] = w1_one[...]
-    wp_all[me.f] = w_proj[...]
-    wqf[me.f] = w_qkv[...]
-    mine = pl.ds(pl.multiple_of(me.j * 64, 64), 64)
-    w2_all[me.f] = w_fc2[mine]
     all_met()
 
     gather = Gather16(wire, me, nrm)
@@ -430,8 +491,31 @@
         got_v.append(wire.send(v_all.at[me.s], v_all.at[me.s], (me.f, peer)))
     half = pl.ds(pl.multiple_of(me.c * 64, 64), 64)
 
-    far_own = None
+    wq_all[me.f] = wq_one[...]
+    for f in range(0, 8, 2):
+        pair = [half_of(me.c, w_fc1[:, lanes(g * 512 + me.y * 128)]) for g in (f, f + 1)]
+        w1_one[:, f * 64 : (f + 2) * 64] = jnp.concatenate(pair, axis=1)
+    w1_all[me.f] = w1_one[...]
+    own_wp = pltpu.make_async_copy(w_proj, wp_all.at[me.f], own_sem.at[0])
+    own_wp.start()
+    wqf[me.f] = w_qkv[...]
+    mine = pl.ds(pl.multiple_of(me.j * 64, 64), 64)
+    own_w2 = pltpu.make_async_copy(w_fc2.at[mine], w2_all.at[me.f], own_sem.at[1])
+    own_w2.start()
     ready = {}
+
+    fan_w1 = Fan(wire, me, w1_one, lambda f: w1_all.at[f])
+    fan_w2 = Fan(wire, me, w_fc2.at[mine], lambda f: w2_all.at[f])
+    fan_wqf = Fan(wire, me, w_qkv.at[half], lambda f: wqf.at[f, half])
+
+    def more_weights():
+        own_wp.wait()
+        own_w2.wait()
+        ready["wp"] = to_fsdp(
+            wire, me, lambda p: w_proj.at[half], lambda f: wp_all.at[f, half]
+        )
+        fan_w1.start()
+        fan_w2.start()
 
     def prepare():
         arrived(got_pv)
@@ -446,10 +530,6 @@
         own = half_of(me.c, pv_all[me.chip].astype(F32))
         zero = jnp.zeros((1, 64), F32)
         ready["bias"] = shifts + jnp.concatenate([own[4:5], zero, own[5:6], zero], axis=1)
-        ready["wp"] = to_fsdp(
-            wire, me, lambda p: w_proj.at[half], lambda f: wp_all.at[f, half]
-        )
-        ready["w1"] = to_fsdp(wire, me, lambda p: w1_one, lambda f: w1_all.at[f])
         arrived(got_v)
         flags = v_all[:, 0, :].astype(F32)
         flags = jnp.concatenate([flags, jnp.zeros((112, 128), F32)], axis=0).T
@@ -464,8 +544,6 @@
     v_ext = jnp.where(ext_lane < 3, 1.0, 0.0).astype(BF16)
 
     def project(slot):
-        if not ready:
-            prepare()
         qkv = dot(nrm[slot], wq_use[...]) + ready["bias"]
         rows = pl.ds(pl.multiple_of(slot * 128, 128), 128)
         query = (qkv[:, :64].astype(BF16) * 0.125).astype(BF16)
@@ -473,11 +551,10 @@
         ka[rows, :64] = qkv[:, 64:128].astype(BF16)
         va[rows, :] = jnp.concatenate([qkv[:, 128:192].astype(BF16), v_ext], axis=1)
 
-    gather.run(project)
+    gather.run(more_weights, prepare, project)
     grd[me.j] = (full_row(pv_all, 9) * gout[...].astype(F32)).astype(BF16)
     grad_gather = Gather8(wire, me, grd)
     grad_gather.start()
-    got_w2 = to_fsdp(wire, me, lambda p: w_fc2.at[mine], lambda f: w2_all.at[f])
 
     heads_out = Scatter(me, as_, ar_, om, at)
     out_lane = lax.broadcasted_iota(jnp.int32, (256, 128), 1)
@@ -502,14 +579,19 @@
         heads_out.send(k)
         return carry
 
+    fan_w1.relay_near()
+    fan_w2.relay_near()
     lax.fori_loop(0, 2, attend_send, 0)
     grad_gather.relay()
+    fan_w1.relay_far()
+    fan_w2.relay_far()
     lax.fori_loop(2, 5, attend_send, 0)
     grad_gather.middle()
     lax.fori_loop(5, 7, attend_send, 0)
     grad_gather.last()
     arrived(ready["wp"])
     swap = [wire.send(wp_all.at[f, half], wp_all.at[f, half], me.core) for f in range(8)]
+    fan_wqf.start()
     attend(7)
     heads_out.keep(wire)
     heads_out.finish()
@@ -532,9 +614,9 @@
     gather.middle()
     attn_gather.start()
     gather.last()
-    arrived(ready["w1"])
-    arrived(got_w2)
-    got_wqf = to_fsdp(wire, me, lambda p: w_qkv.at[half], lambda f: wqf.at[f, half])
+    fan_w1.finish()
+    fan_w2.finish()
+    fan_wqf.relay_near()
     bias_one = jnp.concatenate(
         [pv_all[f].astype(F32)[10:11, :64] for f in range(8)], axis=1
     )
@@ -558,17 +640,20 @@
         return carry + column_sum(grad_pre.astype(F32))
 
     db1[...] = lax.fori_loop(0, 4, feed, jnp.zeros((1, 512), F32))
+    fan_w1.settle()
+    fan_w2.settle()
     reduce = Reduce8(wire, me, gn, r_core, r_far, r_near)
     reduce.start()
+    fan_wqf.relay_far()
     reduce.far()
     attn_gather.relay()
     dw2[...] = dot(act[...], grd[...].reshape(1024, 1024), TN).astype(BF16).reshape(8, 64, 1024)
     reduce.near()
-    got = to_fsdp(wire, me, lambda p: dw2.at[p], lambda f: r2.at[f])
+    fan_dw2 = FanIn(wire, me, dw2, r2)
+    fan_dw2.start()
     dw1[...] = dot(nmg[...].reshape(1024, 1024), gpre[...], TN).astype(BF16).reshape(8, 128, 512)
-    got += to_fsdp(wire, me, lambda p: dw1.at[p], lambda f: r1.at[f])
-    r1[me.f] = dw1[me.f]
-    r2[me.f] = dw2[me.f]
+    fan_dw1 = FanIn(wire, me, dw1, r1)
+    fan_dw1.start()
     cotangent = reduce.result()
     grad_middle = gout[...].astype(F32) + norm_back(cotangent, gain, normed, inverse)
     gmid[...] = grad_middle
@@ -619,6 +704,10 @@
         wide = jnp.where(lane == 67, l3, wide)
         qb[rows, :] = wide.astype(BF16)
         kt[:, rows] = ka[rows, :].astype(F32).T.astype(BF16)
+    for f in range(8):
+        weight = wq_all[f].astype(F32)
+        wqt[f, :128] = weight[:, :128].T.astype(BF16)
+        wqt[f, 128:] = weight[:, 128:].T[:64].astype(BF16)
     dk[...] = jnp.zeros_like(dk)
     dv[...] = jnp.zeros_like(dv)
 
@@ -647,7 +736,7 @@
         dk[...] += dot(scores, query)
         turned = dot(kt[...], scores)
         grad_query = (turned.T[:, :64] * 0.125).astype(BF16)
-        dq[rows, :64] = grad_query
+        dqt[:64, rows] = (turned[:64] * 0.125).astype(BF16)
         for e in range(2):
             qm[chip * 2 + e] = fold(grad_query[e * 128 : (e + 1) * 128])
 
@@ -663,16 +752,13 @@
     for f in range(8):
         tok_cols = atg[:, :, f * 128 : (f + 1) * 128].reshape(1024, 128)
         dwp[f] = dot(tok_cols, gac[...].reshape(1024, 128), TN).astype(BF16)
-    got += to_fsdp(wire, me, lambda p: dwp.at[p], lambda f: rp.at[f])
+    fan_dw2.forward()
+    fan_dw1.forward()
+    got = to_fsdp(wire, me, lambda p: dwp.at[p], lambda f: rp.at[f])
     rp[me.f] = dwp[me.f]
-    arrived(got_wqf)
+    lax.fori_loop(3, 6, back_send, 0)
+    fan_wqf.finish()
     swap = [wire.send(wqf.at[f, half], wqf.at[f, half], me.core) for f in range(8)]
-    lax.fori_loop(3, 6, back_send, 0)
-    arrived(got)
-    x1[0] = eight(r1).astype(BF16)
-    x2[0] = eight(r2).astype(BF16)
-    xp[0] = eight(rp).astype(BF16)
-    crossed = [wire.send(x.at[0], x.at[1], me.xpart) for x in (x1, x2, xp)]
     lax.fori_loop(6, 7, back_send, 0)
     back(7)
     queries_out.keep(wire)
@@ -680,41 +766,47 @@
     for blk in range(16):
         rows = slice(blk * 128, (blk + 1) * 128)
         grad_key, grad_value = dk[rows, :64].astype(BF16), dv[rows, :64].astype(BF16)
-        kvm[blk] = jnp.concatenate([grad_key, grad_value], axis=1)
-        dq[rows, 64:128] = grad_key
-        dq[rows, 128:] = jnp.concatenate([grad_value, jnp.zeros((128, 64), BF16)], axis=1)
+        pair = jnp.concatenate([grad_key, grad_value], axis=1)
+        kvm[blk] = pair
+        dqt[64:, rows] = pair.astype(F32).T.astype(BF16)
     got_kv = []
     for step in range(1, 16):
         peer = (me.s + step) % 16
         got_kv.append(wire.send(kvm.at[peer], kvin.at[me.s], (me.f, peer)))
     kvin[me.s] = kvm[me.s]
 
+    arrived(got)
+    x1[0] = fan_dw1.result().astype(BF16)
+    x2[0] = fan_dw2.result().astype(BF16)
+    xp[0] = eight(rp).astype(BF16)
+    crossed = [wire.send(x.at[0], x.at[1], me.xpart) for x in (x1, x2, xp)]
+
     mlp_out = mlp.result() + full_row(pv_all, 7)
     res[...] = (mid[...] + full_row(pv_all, 9) * mlp_out).astype(BF16)
     vec[9:10, :] = column_sum(gout[...].astype(F32) * mlp_out)
-    sums = column_sum(dq[...].astype(F32))
+    sums = jnp.sum(dqt[...].astype(F32), axis=1, keepdims=True)
+    turned = jnp.broadcast_to(sums, (192, 128))
+    turned = jnp.concatenate([turned, jnp.zeros((64, 128), F32)], axis=0)
+    sum_q, sum_v = turned[:128].T[0:1, :64], turned[128:].T[0:1, :64]
     got_q, got_vec = [], []
     for step in range(1, 9):
         f = (me.f + step) % 8
-        cols = columns(pv_all, f)
-        product = dot(nrm[:, :, lanes(f * 128)].reshape(2048, 128), dq[...], TN)
-        grad_wq = product * cols[:, 0:1] + cols[:, 2:3] * sums
-        weight = wq_all[f].astype(F32)
-        first = jnp.sum(weight * product, axis=1, keepdims=True)
-        second = jnp.sum(weight * sums, axis=1, keepdims=True)
-        turned = jnp.where(lane == 0, first, jnp.where(lane == 1, second, 0.0)).T
+        own = pv_all[f].astype(F32)
+        product = dot(dqt[...], nrm[:, :, lanes(f * 128)].reshape(2048, 128))
+        grad_wq = product * own[0:1] + sums * own[2:3]
+        weight = wqt[f].astype(F32)
         rows = vec[:, lanes(f * 128)]
         piece = half_of(f % 2, db1[:, lanes((f // 2) * 128)])
         bias = beside(me.c, piece)
         here = me.chip == f
         packed = jnp.concatenate(
             [
-                turned[0:1],
+                column_sum(weight * product),
                 rows[1:2],
-                turned[1:2],
+                column_sum(weight * sums),
                 rows[3:4],
-                jnp.where(here, beside(me.c, sums[:, :64]), 0.0),
-                jnp.where(here, beside(me.c, sums[:, 128:192]), 0.0),
+                jnp.where(here, beside(me.c, sum_q), 0.0),
+                jnp.where(here, beside(me.c, sum_v), 0.0),
                 rows[6:10],
                 *[jnp.where(me.y == y, bias, 0.0) for y in range(4)],
                 jnp.zeros((2, 128), F32),
@@ -765,20 +857,8 @@
     for gather in gathers:
         gather.last()
     gather_q.run()
-    for part in range(3):
-        cols = slice(part * 64, (part + 1) * 64)
-        for k in range(8):
-            pair = jnp.concatenate([gq[2 * k, :, cols], gq[2 * k + 1, :, cols]], axis=1)
-            o_qkv[:, part * 1024 + k * 128 : part * 1024 + (k + 1) * 128] = pair
     for gather in gathers:
         gather.finish()
-    for j in range(8):
-        o_proj[:, j * 128 : (j + 1) * 128] = gp[j]
-    for f in range(8):
-        cols = slice(f * 64, (f + 1) * 64)
-        for k in range(4):
-            pair = jnp.concatenate([w1_all[2 * k, :, cols], w1_all[2 * k + 1, :, cols]], axis=1)
-            o_fc1[:, f * 512 + k * 128 : f * 512 + (k + 1) * 128] = pair
     arrived(got_vq)
     total = vq[0]
     for s in range(1, 16):
@@ -790,12 +870,50 @@
 OUTS = (
     ((128, 1024), BF16),
     ((128, 1024), F32),
-    ((128, 3072), BF16),
-    ((128, 1024), BF16),
-    ((128, 4096), BF16),
+    ((16, 192, 128), BF16),
+    ((8, 128, 128), BF16),
+    ((8, 128, 512), BF16),
     ((8, 64, 1024), BF16),
     ((16, 128), F32),
 )
+GRADS = (
+    ((128, 1024), BF16),
+    ((128, 1024), F32),
+    ((128, 3072), F32),
+    ((128, 1024), F32),
+    ((128, 4096), F32),
+    ((512, 1024), F32),
+    ((2, 128), F32),
+    ((6, 128), F32),
+    ((2, 128), F32),
+    ((4, 128), F32),
+)
+
+
+def lay_out(res, gtok, gq, gp, g1, g2, vec, o_res, o_tok, o_qkv, o_proj, o_fc1, o_fc2, *o_vecs):
+    o_res[...] = res[...]
+    o_tok[...] = gtok[...]
+    for part in range(3):
+        rows = slice(part * 64, (part + 1) * 64)
+        for k in range(8):
+            pair = jnp.concatenate([gq[2 * k, rows, :], gq[2 * k + 1, rows, :]], axis=0)
+            at = part * 1024 + k * 128
+            o_qkv[:, at : at + 128] = pair.astype(F32).T
+    for j in range(8):
+        o_proj[:, j * 128 : (j + 1) * 128] = gp[j].astype(F32)
+        o_fc2[j * 64 : (j + 1) * 64, :] = g2[j].astype(F32)
+    for f in range(8):
+        cols = slice(f * 64, (f + 1) * 64)
+        for k in range(4):
+            pair = jnp.concatenate([g1[2 * k, :, cols], g1[2 * k + 1, :, cols]], axis=1)
+            at = f * 512 + k * 128
+            o_fc1[:, at : at + 128] = pair.astype(F32)
+    row = 0
+    for out in o_vecs:
+        out[...] = vec[row : row + out.shape[0], :]
+        row += out.shape[0]
+
+
 SCRATCH = (
     ((16, 128, 1024), BF16),
     ((8, 128, 1024), BF16),
@@ -806,7 +924,6 @@
     ((1024, 256), BF16),
     ((8, 128, 1024), BF16),
     ((128, 512), BF16),
-    ((8, 128, 512), BF16),
     ((8, 128, 3072), BF16),
     ((2048, 128), BF16),
     ((2048, 128), BF16),
@@ -838,7 +955,8 @@
     ((128, 2048), BF16),
     ((2048, 128), F32),
     ((2048, 128), F32),
-    ((2048, 256), BF16),
+    ((192, 2048), BF16),
+    ((8, 192, 128), BF16),
     ((16, 64, 128), BF16),
     ((16, 64, 128), BF16),
     ((16, 128, 128), BF16),
@@ -853,10 +971,8 @@
     ((2, 128, 512), BF16),
     ((2, 64, 1024), BF16),
     ((2, 128, 128), BF16),
-    ((8, 128, 128), BF16),
-    ((8, 128, 256), BF16),
-    ((8, 128, 256), BF16),
-    ((16, 128, 256), BF16),
+    ((8, 192, 128), BF16),
+    ((8, 192, 128), BF16),
     ((8, 16, 128), F32),
     ((8, 16, 128), F32),
     ((16, 16, 128), F32),
@@ -868,12 +984,13 @@
     tokens, image_ids, valid, w_qkv, w_proj, w_fc1, w_fc2,
     norm_gain, shifts, layer_scale, fc1_bias, grad_out,
 ):
-    semaphores = [pltpu.SemaphoreType.DMA((n,)) for n in (COPIES, COPIES, 14, 14, 14, 14)]
+    semaphores = [pltpu.SemaphoreType.DMA((n,)) for n in (COPIES, COPIES, 14, 14, 14, 14, 2)]
     whole = pl.BlockSpec(memory_space=pltpu.VMEM)
-    res, gtok, g_qkv, g_proj, g_fc1, g_fc2, g_vec = pl.pallas_call(
+    held = pl.BlockSpec(memory_space=pl.ANY)
+    shares = pl.pallas_call(
         layer,
         out_shape=[jax.ShapeDtypeStruct(shape, dtype) for shape, dtype in OUTS],
-        in_specs=[whole] * 11,
+        in_specs=[whole] * 4 + [held, whole, held] + [whole] * 4,
         out_specs=[whole] * len(OUTS),
         scratch_shapes=[pltpu.VMEM(shape, dtype) for shape, dtype in SCRATCH] + semaphores,
         name="layer",
@@ -884,18 +1001,15 @@
         tokens, grad_out, valid.reshape(1, 128), w_qkv[0], w_proj[0], w_fc1[0], w_fc2[0],
         norm_gain[0], shifts[0], layer_scale[0], fc1_bias,
     )
-    return (
-        res,
-        gtok,
-        g_qkv[None].astype(F32),
-        g_proj[None].astype(F32),
-        g_fc1[None].astype(F32),
-        g_fc2.reshape(1, 512, 1024).astype(F32),
-        g_vec[None, 0:2],
-        g_vec[None, 2:8],
-        g_vec[None, 8:10],
-        g_vec[10:14].reshape(1, 512),
-    )
+    outs = pl.pallas_call(
+        lay_out,
+        out_shape=[jax.ShapeDtypeStruct(shape, dtype) for shape, dtype in GRADS],
+        in_specs=[whole] * len(OUTS),
+        out_specs=[whole] * len(GRADS),
+        name="lay_out",
+        compiler_params=pltpu.CompilerParams(vmem_limit_bytes=VMEM_LIMIT),
+    )(*shares)
+    return (*outs[:2], *[out[None] for out in outs[2:9]], outs[9].reshape(1, 512))
 
 
 def solution(mesh):

time: 209 us -> 163 us (0.78)
  Pallas kernels: 196 us -> 161 us
  other arithmetic: 6.45 us -> 0 us
  local copies, waits for them, and re-layouts: 5.38 us -> 1.25 us
    pallas_call x1, Pallas kernels: 196 us -> 156 us  [body(): pl.pallas_call(layer, out_shape=[jax.ShapeDtypeStruct(shape, dtype) for s...]
    convert_element_type x4 -> x0, other arithmetic: 6.45 us -> none  [the longest x1 2.79 us: body(): g_fc2.reshape(1, 512, 1024).astype(F32)]
    pallas_call x0 -> x1, Pallas kernels: none -> 5.64 us  [body(): pl.pallas_call(lay_out, out_shape=[jax.ShapeDtypeStruct(shape, dtype) for...]
where the time goes in v3:
time: 163 us
  Pallas kernels  161 us (99%)
    pallas_call x1, Pallas kernels, body(): pl.pallas_call(layer, out_shape=[jax.ShapeDtypeStruct(shape, dtype) for s...  156 us
    pallas_call x1, Pallas kernels, body(): pl.pallas_call(lay_out, out_shape=[jax.ShapeDtypeStruct(shape, dtype) for...  5.64 us

profile of v3, /device:TPU:1, one launch (start us, length us, event | category | flops | bytes accessed | tf_op | source)
XLA Modules:
  0.0 163.2 jit_solution(1248185995049375218)
XLA Ops:
  0.6 155.7 %layer.1 = (bf16[128,1024]{1,0:T(8,128)(2,1)}, f32[128,1024]{1,0:T(8,128)}, bf16[16,192,128]{2,1,0:T(8,128)(2,1)}, bf16[8,128,128]{2,1,0:T(8,128)(2,1)}, bf16[8,...) custom-call(bf16[128,1024]{1,0:T(8,128)(2,1)} %tok.1, bf16[128,1024]{1,0:T(8,128)(2,1)} %gout.1, ...), custom_call_target="tpu_custom_call" | custom-call | tf_op jit(solution)/shard_map/layer/pallas_call | solution.py:990
  156.3 5.6 %lay_out.1 = (bf16[128,1024]{1,0:T(8,128)(2,1)}, f32[128,1024]{1,0:T(8,128)}, f32[128,3072]{1,0:T(8,128)}, f32[128,1024]{1,0:T(8,128)}, f32[128,4096]{1,0:T(8,12...) custom-call(bf16[128,1024]{1,0:T(8,128)(2,1)} %get-tuple-element.27., ...), custom_call_target="tpu_custom_call" | custom-call | tf_op jit(solution)/shard_map/lay_out/pallas_call | solution.py:1004
  161.9 1.3 copy.21

commit v4 on v3

--- a/solution.py
+++ b/solution.py
@@ -337,12 +337,13 @@
         self.from_core, self.from_far, self.from_near = from_core, from_far, from_near
         self.order = (me.yo, me.yp, me.ym, me.y)
 
-    def start(self):
-        me = self.me
-        self.cores = []
-        for d, y in enumerate(self.order):
-            src = self.part.at[y * 2 + 1 - me.c]
-            self.cores.append(self.wire.send(src, self.from_core.at[d], me.core))
+        self.cores = {}
+        h = from_core.shape[1] // 2
+        self.head, self.tail = pl.ds(0, h), pl.ds(h, h)
+
+    def start(self, d):
+        src = self.part.at[self.order[d] * 2 + 1 - self.me.c]
+        self.cores[d] = self.wire.send(src, self.from_core.at[d], self.me.core)
 
     def combine(self, d):
         self.cores[d].wait_recv()
@@ -352,11 +353,12 @@
 
     def far(self):
         w, me, acc = self.wire, self.me, self.from_core
-        h = acc.shape[1] // 2
-        self.head, self.tail = pl.ds(0, h), pl.ds(h, h)
         self.combine(0)
         self.f_up = w.send(acc.at[0, self.head], self.from_far.at[0], me.up)
         self.f_down = w.send(acc.at[0, self.tail], self.from_far.at[1], me.down)
+
+    def near_halves(self):
+        w, me, acc = self.wire, self.me, self.from_core
         self.combine(1)
         self.n_up = [w.send(acc.at[1, self.tail], self.from_near.at[0, self.tail], me.up)]
         self.combine(2)
@@ -611,18 +613,15 @@
     attn_gather = Gather8(wire, me, atg)
     grad_gather.finish()
     gather.relay()
-    gather.middle()
-    attn_gather.start()
-    gather.last()
     fan_w1.finish()
     fan_w2.finish()
     fan_wqf.relay_near()
     bias_one = jnp.concatenate(
         [pv_all[f].astype(F32)[10:11, :64] for f in range(8)], axis=1
     )
-    gather.finish()
-
-    def feed(b, carry):
+    reduce = Reduce8(wire, me, gn, r_core, r_far, r_near)
+
+    def feed(b):
         two = pl.ds(2 * b, 2)
         rows = pl.ds(pl.multiple_of(b * 256, 256), 256)
         w1 = w1_all[...].reshape(1024, 512)
@@ -637,13 +636,26 @@
         grad_pre = (grad_act * slope).astype(BF16)
         gpre[rows, :] = grad_pre
         gn[two] = dot(grad_pre, w1, NT).astype(BF16).reshape(2, 128, 1024)
-        return carry + column_sum(grad_pre.astype(F32))
-
-    db1[...] = lax.fori_loop(0, 4, feed, jnp.zeros((1, 512), F32))
+        return column_sum(grad_pre.astype(F32))
+
+    gather.cores[0].wait_recv()
+    bias_sum = feed(me.y)
+    reduce.start(3)
+    gather.middle()
+    attn_gather.start()
+    gather.cores[1].wait_recv()
+    bias_sum += feed(me.ym)
+    reduce.start(2)
+    gather.last()
+    gather.cores[2].wait_recv()
+    bias_sum += feed(me.yp)
+    reduce.start(1)
+    reduce.near_halves()
+    gather.cores[3].wait_recv()
+    db1[...] = bias_sum + feed(me.yo)
+    reduce.start(0)
     fan_w1.settle()
     fan_w2.settle()
-    reduce = Reduce8(wire, me, gn, r_core, r_far, r_near)
-    reduce.start()
     fan_wqf.relay_far()
     reduce.far()
     attn_gather.relay()
@@ -674,7 +686,8 @@
         got_gac.append(wire.send(gat.at[:, lanes(peer * 128)], gac.at[me.j], device))
     gac[me.j] = gat[:, lanes(me.j * 128)]
     mlp = Reduce8(wire, me, mp, m_core, m_far, m_near)
-    mlp.start()
+    for d in range(4):
+        mlp.start(d)
     zero = jnp.zeros((1, 1024), F32)
     vec[...] = jnp.concatenate(
         [
@@ -694,6 +707,7 @@
     attn_gather.middle()
     attn_gather.last()
     mlp.far()
+    mlp.near_halves()
     lane = lax.broadcasted_iota(jnp.int32, (128, 128), 1)
     for blk in range(16):
         rows = slice(blk * 128, (blk + 1) * 128)
@@ -780,7 +794,6 @@
     x2[0] = fan_dw2.result().astype(BF16)
     xp[0] = eight(rp).astype(BF16)
     crossed = [wire.send(x.at[0], x.at[1], me.xpart) for x in (x1, x2, xp)]
-
     mlp_out = mlp.result() + full_row(pv_all, 7)
     res[...] = (mid[...] + full_row(pv_all, 9) * mlp_out).astype(BF16)
     vec[9:10, :] = column_sum(gout[...].astype(F32) * mlp_out)
@@ -886,32 +899,65 @@
     ((2, 128), F32),
     ((6, 128), F32),
     ((2, 128), F32),
-    ((4, 128), F32),
+    ((1, 512), F32),
 )
 
 
-def lay_out(res, gtok, gq, gp, g1, g2, vec, o_res, o_tok, o_qkv, o_proj, o_fc1, o_fc2, *o_vecs):
-    o_res[...] = res[...]
-    o_tok[...] = gtok[...]
+def lay_out(*refs):
+    count = len(OUTS)
+    given, outs = refs[:count], refs[count : count + len(GRADS)]
+    scratch, sem = refs[count + len(GRADS) : -1], refs[-1]
+    held, ready = scratch[:count], scratch[count:]
+    copies = []
+    for k in (5, 4, 2, 3, 6, 0, 1):
+        copies.append(pltpu.make_async_copy(given[k], held[k], sem.at[k]))
+        copies[-1].start()
+
+    def store(k):
+        src = held[k] if k < 2 else ready[k - 2]
+        copies.append(pltpu.make_async_copy(src, outs[k], sem.at[count + k]))
+        copies[-1].start()
+
+    gq, gp, g1, g2, vec = held[2:]
+    o_qkv, o_proj, o_fc1, o_fc2 = ready[:4]
+    copies[0].wait()
+    for j in range(8):
+        o_fc2[j * 64 : (j + 1) * 64, :] = g2[j].astype(F32)
+    store(5)
+    copies[1].wait()
+    for f in range(8):
+        cols = slice(f * 64, (f + 1) * 64)
+        for k in range(4):
+            pair = jnp.concatenate([g1[2 * k, :, cols], g1[2 * k + 1, :, cols]], axis=1)
+            at = f * 512 + k * 128
+            o_fc1[:, at : at + 128] = pair.astype(F32)
+    store(4)
+    copies[2].wait()
     for part in range(3):
         rows = slice(part * 64, (part + 1) * 64)
         for k in range(8):
             pair = jnp.concatenate([gq[2 * k, rows, :], gq[2 * k + 1, rows, :]], axis=0)
             at = part * 1024 + k * 128
             o_qkv[:, at : at + 128] = pair.astype(F32).T
+    store(2)
+    copies[3].wait()
     for j in range(8):
         o_proj[:, j * 128 : (j + 1) * 128] = gp[j].astype(F32)
-        o_fc2[j * 64 : (j + 1) * 64, :] = g2[j].astype(F32)
-    for f in range(8):
-        cols = slice(f * 64, (f + 1) * 64)
-        for k in range(4):
-            pair = jnp.concatenate([g1[2 * k, :, cols], g1[2 * k + 1, :, cols]], axis=1)
-            at = f * 512 + k * 128
-            o_fc1[:, at : at + 128] = pair.astype(F32)
+    store(3)
+    copies[4].wait()
     row = 0
-    for out in o_vecs:
-        out[...] = vec[row : row + out.shape[0], :]
-        row += out.shape[0]
+    for k in range(6, 9):
+        size = GRADS[k][0][0]
+        ready[k - 2][...] = vec[row : row + size, :]
+        row += size
+        store(k)
+    ready[7][...] = jnp.concatenate([vec[k : k + 1, :] for k in range(row, row + 4)], axis=1)
+    store(9)
+    for k in (0, 1):
+        copies[5 + k].wait()
+        store(k)
+    for copy in copies[7:]:
+        copy.wait()
 
 
 SCRATCH = (
@@ -1004,12 +1050,14 @@
     outs = pl.pallas_call(
         lay_out,
         out_shape=[jax.ShapeDtypeStruct(shape, dtype) for shape, dtype in GRADS],
-        in_specs=[whole] * len(OUTS),
-        out_specs=[whole] * len(GRADS),
+        in_specs=[held] * len(OUTS),
+        out_specs=[held] * len(GRADS),
+        scratch_shapes=[pltpu.VMEM(shape, dtype) for shape, dtype in OUTS + GRADS[2:]]
+        + [pltpu.SemaphoreType.DMA((len(OUTS) + len(GRADS),))],
         name="lay_out",
         compiler_params=pltpu.CompilerParams(vmem_limit_bytes=VMEM_LIMIT),
     )(*shares)
-    return (*outs[:2], *[out[None] for out in outs[2:9]], outs[9].reshape(1, 512))
+    return (*outs[:2], *[out[None] for out in outs[2:9]], outs[9])
 
 
 def solution(mesh):

time: 163 us -> 159 us (0.975)
  Pallas kernels: 161 us -> 157 us
    pallas_call x1, Pallas kernels: 156 us -> 152 us  [body(): pl.pallas_call(layer, out_shape=[jax.ShapeDtypeStruct(shape, dtype) for s...]
where the time goes in v4:
time: 159 us
  Pallas kernels  157 us (99%)
    pallas_call x1, Pallas kernels, body(): pl.pallas_call(layer, out_shape=[jax.ShapeDtypeStruct(shape, dtype) for s...  152 us
    pallas_call x1, Pallas kernels, body(): pl.pallas_call(lay_out, out_shape=[jax.ShapeDtypeStruct(shape, dtype) for...  4.42 us

profile of v4, /device:TPU:1, one launch (start us, length us, event | category | flops | bytes accessed | tf_op | source)
XLA Modules:
  0.0 158.8 jit_solution(10856290055494223384)
XLA Ops:
  0.6 152.5 %layer.1 = (bf16[128,1024]{1,0:T(8,128)(2,1)}, f32[128,1024]{1,0:T(8,128)}, bf16[16,192,128]{2,1,0:T(8,128)(2,1)}, bf16[8,128,128]{2,1,0:T(8,128)(2,1)}, bf16[8,...) custom-call(bf16[128,1024]{1,0:T(8,128)(2,1)} %tok.1, bf16[128,1024]{1,0:T(8,128)(2,1)} %gout.1, ...), custom_call_target="tpu_custom_call" | custom-call | tf_op jit(solution)/shard_map/layer/pallas_call | solution.py:1036
  153.1 4.4 %lay_out.1 = (bf16[128,1024]{1,0:T(8,128)(2,1)}, f32[128,1024]{1,0:T(8,128)}, f32[128,3072]{1,0:T(8,128)}, f32[128,1024]{1,0:T(8,128)}, f32[128,4096]{1,0:T(8,12...) custom-call(bf16[128,1024]{1,0:T(8,128)(2,1)} %get-tuple-element.27., ...), custom_call_target="tpu_custom_call" | custom-call | tf_op jit(solution)/shard_map/lay_out/pallas_call | solution.py:1050
  157.6 1.3 copy.21
